TPU v7x, 128 devices: a whole 4x4x4 slice. The times are simulated.
128 devices in a mesh: rep: 16 (over z, y_lo, core), node: 8 (over x, y_hi).
Axes of the slice: x: 4, y: 4 (y_hi: 2, y_lo: 2; y = y_hi * 2 + y_lo), z: 4, core: 2. Of those that a mesh axis runs over, the one named last changes fastest.
Arguments:
- tokens: bfloat16 [4096, 4096], P('node', 'rep'), may hold values from -6 to 6
- cotangent: bfloat16 [4096, 4096], P('node'), may hold values from -6 to 6
- gate_weight: bfloat16 [4096, 14336], P('node', 'rep'), may hold values from -0.125 to 0.125
- up_weight: bfloat16 [4096, 14336], P('node', 'rep'), may hold values from -0.09375 to 0.09375
- down_weight: bfloat16 [14336, 4096], P('rep', 'node'), may hold values from -0.046875 to 0.046875
Outputs:
- d_tokens: bfloat16 [4096, 4096], P('node', 'rep')
- grad_gate: bfloat16 [4096, 14336], P('node', 'rep')
- grad_up: bfloat16 [4096, 14336], P('node', 'rep')
- grad_down: bfloat16 [14336, 4096], P('rep', 'node')
All inputs are finite; a program needn't handle non-finite values.
Results may differ from a plain program's by a relative error of at most 0.015.
Values may be sent and summed in bfloat16 or wider, within the bound.
No kernel may reach another device: no remote copies, remote signals or barrier semaphores. Data moves between devices by JAX's collectives and lax.ppermute only.
A program may use at most 192 MiB of HBM per device.

v0:
```python
import jax
import jax.numpy as jnp
from jax import lax
from jax.sharding import PartitionSpec as P


def per_device(tokens, cotangent, gate_weight, up_weight, down_weight):
    feats = lax.all_gather(tokens, "rep", axis=1, tiled=True)
    gate_full, up_full = (
        lax.all_gather(gate_weight, "node", axis=0, tiled=True),
        lax.all_gather(up_weight, "node", axis=0, tiled=True),
    )
    gate = jnp.dot(feats, gate_full, preferred_element_type=jnp.float32)
    up = jnp.dot(feats, up_full, preferred_element_type=jnp.float32)
    sig = jax.nn.sigmoid(gate)
    hidden = (gate * sig * up).astype(jnp.bfloat16)
    width_dev = gate_weight.shape[1]
    d_hidden = lax.dot_general(
        cotangent,
        lax.all_gather(down_weight, "node", axis=1, tiled=True),
        (((1,), (1,)), ((), ())),
        preferred_element_type=jnp.float32,
    )
    d_gate = (d_hidden * up * sig * (1.0 + gate * (1.0 - sig))).astype(jnp.bfloat16)
    d_up = (d_hidden * gate * sig).astype(jnp.bfloat16)
    partial_x = lax.dot_general(
        d_gate, gate_full, (((1,), (1,)), ((), ())), preferred_element_type=jnp.float32
    )
    partial_x = partial_x + lax.dot_general(
        d_up, up_full, (((1,), (1,)), ((), ())), preferred_element_type=jnp.float32
    )
    d_tokens = lax.psum_scatter(partial_x, "rep", scatter_dimension=1, tiled=True).astype(
        jnp.bfloat16
    )
    both_grads = jnp.concatenate([d_gate, d_up], axis=1)
    summed = lax.psum_scatter(
        lax.dot_general(
            feats, both_grads, (((0,), (0,)), ((), ())), preferred_element_type=jnp.float32
        ).astype(jnp.bfloat16),
        "node",
        scatter_dimension=0,
        tiled=True,
    ).astype(jnp.float32)
    grad_gate = summed[:, :width_dev]
    grad_up = summed[:, width_dev:]
    down_term = lax.dot_general(
        hidden, cotangent, (((0,), (0,)), ((), ())), preferred_element_type=jnp.float32
    )
    grad_down = lax.psum_scatter(
        down_term.astype(jnp.bfloat16), "node", scatter_dimension=1, tiled=True
    )
    return (d_tokens, grad_gate.astype(jnp.bfloat16), grad_up.astype(jnp.bfloat16), grad_down)


def solution(mesh):
    placed = (
        P("node", "rep"),
        P("node", None),
        P("node", "rep"),
        P("node", "rep"),
        P("rep", "node"),
    )
    return jax.shard_map(
        per_device,
        mesh=mesh,
        in_specs=placed,
        out_specs=(P("node", "rep"), P("node", "rep"), P("node", "rep"), P("rep", "node")),
        check_vma=False,
    )
```

profile of v0, /device:TPU:1, one launch (start us, length us, event | category | flops | bytes accessed | tf_op | source)
XLA Modules:
  0.0 782.2 jit_solution(3754981805423279194)
XLA Ops:
  7.2 0.0 all-gather.7.cloned.1.call-start
  7.2 0.7 all-gather.7.cloned.1.call-update
  7.9 0.0 all-gather.9.cloned.1.call-start
  7.9 0.7 all-gather.9.cloned.1.call-update
  8.6 0.0 all-gather.11.cloned.1.call-start
  8.7 0.7 all-gather.11.cloned.1.call-update
  9.4 0.0 all-gather.5.cloned.1.call-start
  9.4 0.5 all-gather.5.cloned.1.call-update
  10.0 0.0 reduce-scatter.4.cloned.1.call-start
  10.0 48.8 %all-gather.7.cloned.1.call-done = bf16[512,4096]{1,0:T(8,128)(2,1)} async-done(((bf16[512,256]{1,0:T(8,128)(2,1)}), bf16[512,4096]{1,0:T(8,128)(2,1)}) %all-gather.7.cloned.1.call-update) | async-done | bytes 4194320 | tf_op jit(solution)/shard_map/all_gather | solution.py:8
  58.8 100.7 %all-gather.9.cloned.1.call-done = bf16[4096,896]{1,0:T(8,128)(2,1)} async-done(((bf16[512,896]{1,0:T(8,128)(2,1)}), bf16[4096,896]{1,0:T(8,128)(2,1)}) %all-gather.9.cloned.1.call-update) | async-done | bytes 7340048 | tf_op jit(solution)/shard_map/all_gather | solution.py:11
  159.5 10.1 %fusion.8 = f32[512,896]{1,0:T(8,128)} fusion(bf16[512,4096]{1,0:T(8,128)(2,1)} %all-gather.7.cloned.1.call-done, bf16[4096,896]{1,0:T(8,128)(2,1)} %all-gather.9.cloned.1.call-done), kind=kOutput, calls=%fused_computation.15 | convolution fusion | flops 3758096384 | bytes 13369344 | tf_op jit(solution)/shard_map/dot_general | solution.py:14
  169.5 89.5 %all-gather.11.cloned.1.call-done = bf16[4096,896]{1,0:T(8,128)(2,1)} async-done(((bf16[512,896]{1,0:T(8,128)(2,1)}), bf16[4096,896]{1,0:T(8,128)(2,1)}) %all-gather.11.cloned.1.call-update) | async-done | bytes 7340048 | tf_op jit(solution)/shard_map/all_gather | solution.py:10
  259.0 10.1 %fusion.9 = f32[512,896]{1,0:T(8,128)} fusion(bf16[512,4096]{1,0:T(8,128)(2,1)} %all-gather.7.cloned.1.call-done, bf16[4096,896]{1,0:T(8,128)(2,1)} %all-gather.11.cloned.1.call-done), kind=kOutput, calls=%fused_computation.16 | convolution fusion | flops 3758096384 | bytes 13369344 | tf_op jit(solution)/shard_map/dot_general | solution.py:13
  269.1 99.3 %all-gather.5.cloned.1.call-done = bf16[896,4096]{1,0:T(8,128)(2,1)} async-done(((bf16[896,512]{1,0:T(8,128)(2,1)}), bf16[896,4096]{1,0:T(8,128)(2,1)}) %all-gather.5.cloned.1.call-update) | async-done | bytes 7340048 | tf_op jit(solution)/shard_map/all_gather | solution.py:20
  368.4 10.4 %multiply_convert_fusion.1 = (bf16[512,896]{1,0:T(8,128)(2,1)S(1)}, bf16[512,896]{1,0:T(8,128)(2,1)S(1)}) fusion(f32[512,896]{1,0:T(8,128)} %fusion.9, f32[512,896]{1,0:T(8,128)} %fusion.8, bf16[512,4096]{1,0:T(8,128)(2,1)} %param.6, bf16[896,4096]{1,0:T(8,128)(2,1)} %all-gather.5.cloned.1.call-done), kind=kOutput, calls=%fused_computation.8 | convolution fusion | flops 3764060160 | bytes 17039360 | tf_op jit(solution)/shard_map/dot_general | solution.py:18
  378.8 4.8 fusion.10
  383.6 10.0 %convolution_add_fusion = f32[512,4096]{1,0:T(8,128)} fusion(f32[512,4096]{1,0:T(8,128)S(1)} %fusion.10, bf16[512,896]{1,0:T(8,128)(2,1)S(1)} %get-tuple-element.8, bf16[4096,896]{1,0:T(8,128)(2,1)} %all-gather.9.cloned.1.call-done), kind=kOutput, calls=%fused_computation.3 | convolution fusion | flops 3760193536 | bytes 25034752 | tf_op jit(solution)/shard_map/dot_general | solution.py:29
  393.6 0.0 reduce-scatter.4.cloned.1.call-update
  393.6 0.0 reduce-scatter.6.cloned.1.call-start
  393.6 13.3 %fusion = bf16[4096,1792]{0,1:T(8,128)(2,1)} fusion(bf16[512,4096]{1,0:T(8,128)(2,1)} %all-gather.7.cloned.1.call-done, bf16[512,896]{1,0:T(8,128)(2,1)S(1)} %get-tuple-element.8, bf16[512,896]{1,0:T(8,128)(2,1)S(1)} %get-tuple-element.9), kind=kOutput, calls=%fused_computation.1 | convolution fusion | flops 7527202816 | bytes 20709376 | tf_op jit(solution)/shard_map/dot_general | solution.py:37
  407.0 0.0 reduce-scatter.8.cloned.1.call-start
  407.1 1.4 copy-done.1
  408.5 9.9 %convolution_convert_fusion.1 = bf16[896,4096]{1,0:T(8,128)(2,1)} fusion(bf16[512,4096]{1,0:T(8,128)(2,1)} %param.6, f32[512,896]{1,0:T(8,128)S(1)} %copy-done.1, f32[512,896]{1,0:T(8,128)} %fusion.9), kind=kOutput, calls=%fused_computation.2 | convolution fusion | flops 3764518912 | bytes 15204352 | tf_op jit(solution)/shard_map/dot_general | solution.py:46
  418.4 0.0 reduce-scatter.8.cloned.1.call-update
  418.4 71.2 %reduce-scatter.4.cloned.1.call-done = f32[512,256]{1,0:T(8,128)} async-done(((f32[512,4096]{1,0:T(8,128)}), f32[512,256]{1,0:T(8,128)}) %reduce-scatter.4.cloned.1.call-update) | async-done | bytes 524304 | tf_op jit(solution)/shard_map/reduce_scatter | solution.py:32
  489.6 1.8 convert_element_type.26
  491.4 172.4 %reduce-scatter.6.cloned.1.call-done = bf16[512,1792]{0,1:T(8,128)(2,1)} async-done(((bf16[4096,1792]{0,1:T(8,128)(2,1)}), bf16[512,1792]{0,1:T(8,128)(2,1)}) %reduce-scatter.6.cloned.1.call-update) | async-done | bytes 1835024 | tf_op jit(solution)/shard_map/reduce_scatter | solution.py:36
  663.7 1.6 fusion.7
  665.3 1.3 copy.10
  666.6 1.3 copy.9
  667.9 107.5 %reduce-scatter.8.cloned.1.call-done = bf16[896,512]{1,0:T(8,128)(2,1)} async-done(((bf16[896,4096]{1,0:T(8,128)(2,1)}), bf16[896,512]{1,0:T(8,128)(2,1)}) %reduce-scatter.8.cloned.1.call-update) | async-done | bytes 917520 | tf_op jit(solution)/shard_map/reduce_scatter | solution.py:49
  (4 shorter events, 0.0 us)
Async XLA Ops:
  7.2 51.6 %all-gather.7.cloned.1.call-start = ((), (), s32[]{:S(2)}) async-start(), calls=%async_computation.4 | async-start | bytes 4456448 | tf_op jit(solution)/shard_map/all_gather | solution.py:8
  7.9 151.6 %all-gather.9.cloned.1.call-start = ((), (), s32[]{:S(2)}) async-start(), calls=%async_computation.5 | async-start | bytes 8257536 | tf_op jit(solution)/shard_map/all_gather | solution.py:11
  8.6 250.3 %all-gather.11.cloned.1.call-start = ((), (), s32[]{:S(2)}) async-start(), calls=%async_computation.6 | async-start | bytes 8257536 | tf_op jit(solution)/shard_map/all_gather | solution.py:10
  9.4 359.0 %all-gather.5.cloned.1.call-start = ((), (), s32[]{:S(2)}) async-start(), calls=%async_computation.3 | async-start | bytes 8257536 | tf_op jit(solution)/shard_map/all_gather | solution.py:20
  10.0 479.6 %reduce-scatter.4.cloned.1.call-start = ((), (), s32[]{:S(2)}) async-start(), calls=%async_computation.7 | async-start | bytes 8912896 | tf_op jit(solution)/shard_map/reduce_scatter | solution.py:32
  368.4 10.4 %copy-start = (bf16[4096,896]{1,0:T(8,128)(2,1)S(1)}, bf16[4096,896]{1,0:T(8,128)(2,1)}, u32[]{:S(2)}) copy-start(bf16[4096,896]{1,0:T(8,128)(2,1)} %all-gather.11.cloned.1.call-done) | copy-start | bytes 22020100
  393.6 270.1 %reduce-scatter.6.cloned.1.call-start = ((), (), s32[]{:S(2)}) async-start(), calls=%async_computation.8 | async-start | bytes 16515072 | tf_op jit(solution)/shard_map/reduce_scatter | solution.py:36
  407.0 1.5 copy-start.1
  407.0 368.3 %reduce-scatter.8.cloned.1.call-start = ((), (), s32[]{:S(2)}) async-start(), calls=%async_computation.9 | async-start | bytes 8257536 | tf_op jit(solution)/shard_map/reduce_scatter | solution.py:49
Sparse Core Ops, SparseCore 0:
  9.6 49.1 all-gather.6
  61.1 98.3 all-gather.8
  161.8 97.1 all-gather.10
  261.0 107.3 all-gather.4
  393.7 95.8 reduce-scatter.3
  493.4 170.3 reduce-scatter.5
  668.7 106.5 reduce-scatter.7
where the time goes:
time: 782 us
  waiting for transfers between devices  692 us (88%)
  matrix products  68.5 us (9%)
  between operations  14.1 us (2%)
    reduce_scatter x1, waiting for transfers between devices, per_device(): lax.psum_scatter(lax.dot_general(feats, both_grads, (((0,), (0,)), ((), (...  172 us
    reduce_scatter x1, waiting for transfers between devices, per_device(): lax.psum_scatter(down_term.astype(jnp.bfloat16), 'node', scatter_dimensio...  107 us
    all_gather x1, waiting for transfers between devices, per_device(): lax.all_gather(up_weight, 'node', axis=0, tiled=True)  101 us
    all_gather x1, waiting for transfers between devices, per_device(): lax.all_gather(down_weight, 'node', axis=1, tiled=True)  99.3 us
    all_gather x1, waiting for transfers between devices, per_device(): lax.all_gather(gate_weight, 'node', axis=0, tiled=True)  89.5 us
    reduce_scatter x1, waiting for transfers between devices, per_device(): lax.psum_scatter(partial_x, 'rep', scatter_dimension=1, tiled=True)  71.2 us
    all_gather x1, waiting for transfers between devices, per_device(): feats = lax.all_gather(tokens, 'rep', axis=1, tiled=True)  48.8 us
  transfers between devices with their start and end apart: 7, of which 7 were waited for; matrix products, arithmetic and copies ran while one was open for 6% of the time, Pallas kernels for 0%

commit v1 on v0

v1 whole, which is shorter than its diff:
```python
import functools

import jax
import jax.numpy as jnp
from jax import lax
from jax.experimental import pallas as pl
from jax.experimental.pallas import tpu as pltpu
from jax.sharding import Mesh, PartitionSpec as P

BF = jnp.bfloat16
F32 = jnp.float32
SWAP = [(0, 1), (1, 0)]
SPLIT = 512
VMEM = 56 * 2**20


def ring(v, axis, step):
    return lax.ppermute(v, axis, [(i, (i + step) % 4) for i in range(4)])


def sibling(v):
    return lax.ppermute(v, "c", SWAP)


def across(v):
    return lax.ppermute(v, "yh", SWAP)


def beside(v):
    return lax.ppermute(v, "yl", SWAP)


def behind(v):
    return lax.ppermute(v, ("yl", "yh"), [(0, 3), (3, 0), (1, 2), (2, 1)])


def cut(v, i, axis):
    half = v.shape[axis] // 2
    return lax.dynamic_slice_in_dim(v, i * half, half, axis)


def cat(*pieces, axis=0):
    return jnp.concatenate(pieces, axis)


def ordered(first, a, b, axis):
    return jnp.where(first, cat(a, b, axis=axis), cat(b, a, axis=axis))


def after(values, *first):
    return lax.optimization_barrier((tuple(values), first))[0]


def mm(a, b, ca=1, cb=0):
    return lax.dot_general(a, b, (((ca,), (cb,)), ((), ())), preferred_element_type=F32)


def call(body, name, places, operands, specs, out, out_spec, grid, scratch=(), flops=0):
    moved = sum(o.size * o.dtype.itemsize for o in (*operands, *jax.tree.leaves(out)))
    return pl.pallas_call(
        body,
        grid_spec=pltpu.PrefetchScalarGridSpec(
            num_scalar_prefetch=1, grid=grid, in_specs=specs, out_specs=out_spec, scratch_shapes=list(scratch)),
        out_shape=out,
        compiler_params=pltpu.CompilerParams(vmem_limit_bytes=VMEM),
        cost_estimate=pl.CostEstimate(flops=flops // 100, bytes_accessed=moved // 100, transcendentals=0),
        name=name,
    )(places, *operands)


def _copy(places, src, dst):
    dst[...] = src[...]


def columns(v, places, width, height=None):
    rows, n = v.shape[0], places.shape[0]
    return call(_copy, "columns", places, (v,), [pl.BlockSpec((rows, width), lambda i, s: (0, s[i]))],
                jax.ShapeDtypeStruct((height or rows, n * width), v.dtype), pl.BlockSpec((rows, width), lambda i, s: (0, i)), (n,))


def _partial_x(places, x0, x1, x2, x3, w, theirs, mine):
    block = theirs.shape[0]
    c = places[4]
    for out, half in ((theirs, 1 - c), (mine, c)):
        at = pl.ds(pl.multiple_of(half * block, block), block)
        out[...] = sum(mm(x[0, at], w[k * block:(k + 1) * block]) for k, x in enumerate((x0, x1, x2, x3))).astype(out.dtype)


def partial_x(X, W, places):
    depth, n3 = W.shape
    block, n = depth // 4, n3 // 3
    return call(
        _partial_x, "partial_x", places, (X, X, X, X, W),
        [pl.BlockSpec((1, 2 * block, block), lambda i, s, k=k: (s[k], 0, 0)) for k in range(4)]
        + [pl.BlockSpec((depth, n), lambda i, s: (0, i))],
        (jax.ShapeDtypeStruct((block, 2 * n), BF), jax.ShapeDtypeStruct((block, 2 * n), F32)),
        (pl.BlockSpec((block, n), lambda i, s: (0, i)),) * 2, (2,), (), 16 * block * block * n3)


def _partial_c(places, cot, w, theirs, mine):
    block = theirs.shape[0]
    for out, half in ((theirs, 1 - places[0]), (mine, places[0])):
        out[...] = mm(cot[pl.ds(pl.multiple_of(half * block, block), block)], w[...]).astype(out.dtype)


def partial_c(C, W, places):
    depth, n3 = W.shape
    block, n = depth // 4, n3 // 3
    step = n // 2 if n % 512 == 0 else n
    return call(
        _partial_c, "partial_c", places, (C, W),
        [pl.BlockSpec(C.shape, lambda i, s: (0, 0)), pl.BlockSpec((depth, step), lambda i, s: (0, 2 * (n // step) + i))],
        (jax.ShapeDtypeStruct((block, n), BF), jax.ShapeDtypeStruct((block, n), F32)),
        (pl.BlockSpec((block, step), lambda i, s: (0, i)),) * 2, (n // step,), (), 16 * block * block * n)


def _activate(n, places, mine, theirs, mine_d, theirs_d, out):
    total = mine[...] + theirs[...].astype(F32)
    gate, up = total[:, :n], total[:, n:]
    d_hidden = mine_d[...] + theirs_d[...].astype(F32)
    sig = 1.0 / (1.0 + jnp.exp(-gate))
    act = gate * sig
    out[:, :n] = (d_hidden * up * sig * (1.0 + gate * (1.0 - sig))).astype(out.dtype)
    out[:, n:2 * n] = (d_hidden * act).astype(out.dtype)
    out[:, 2 * n:] = (act * up).astype(out.dtype)


def activate(mine, theirs, mine_d, theirs_d, places):
    rows, n = mine_d.shape
    spec = lambda m: pl.BlockSpec((rows // 4, m), lambda i, s: (i, 0))
    return call(functools.partial(_activate, n), "activate", places, (mine, theirs, mine_d, theirs_d),
                [spec(2 * n), spec(2 * n), spec(n), spec(n)],
                jax.ShapeDtypeStruct((rows, 3 * n), BF), spec(3 * n), (4,), (), 30 * rows * n)


def _grads(n, places, xm, xo, cm, co, dm, do, out):
    out[:, :2 * n] = (mm(xm[0], dm[:, :2 * n], 0, 0) + mm(xo[0], do[:, :2 * n], 0, 0)).astype(out.dtype)
    out[:, 2 * n:] = (mm(cm[...], dm[:, 2 * n:], 0, 0) + mm(co[...], do[:, 2 * n:], 0, 0)).astype(out.dtype)


def grads(X, C, mine, other, x_of, c, ks):
    block, n3 = mine.shape
    m = len(ks)
    places = jnp.stack([*(x_of[k] for k in ks), *ks, c]).astype(jnp.int32)
    full = pl.BlockSpec((block, n3), lambda i, s: (0, 0))
    return call(
        functools.partial(_grads, n3 // 3), "grads", places, (X, X, C, C, mine, other),
        [pl.BlockSpec((1, block, block), lambda i, s: (s[i], s[2 * m], 0)),
         pl.BlockSpec((1, block, block), lambda i, s: (s[i], 1 - s[2 * m], 0)),
         pl.BlockSpec((block, block), lambda i, s: (s[2 * m], s[m + i])),
         pl.BlockSpec((block, block), lambda i, s: (1 - s[2 * m], s[m + i])),
         full, full],
        jax.ShapeDtypeStruct((m * block, n3), BF), pl.BlockSpec((block, n3), lambda i, s: (i, 0)), (m,), (), 4 * m * block * block * n3)


def _d_x(m, places, wa, wb, ma, oa, mb, ob, out):
    na, nb = wa.shape[1] // 3 * 2, wb.shape[1] // 3 * 2
    c, block = places[m], ma.shape[0]
    for at, a, b in ((c, ma, mb), (1 - c, oa, ob)):
        total = mm(a[:, :na], wa[:, :na], 1, 1) + mm(b[:, :nb], wb[:, :nb], 1, 1)
        out[pl.ds(pl.multiple_of(at * block, block), block)] = total.astype(out.dtype)


def d_x(WA, WB, A, B, w_of, c, js):
    block, m = A[0].shape[0], len(js)
    places = jnp.stack([*(w_of[j] for j in js), c]).astype(jnp.int32)
    w = lambda v: pl.BlockSpec((block, v.shape[1]), lambda i, s: (s[i], 0))
    full = lambda v: pl.BlockSpec(v.shape, lambda i, s: (0, 0))
    return call(
        functools.partial(_d_x, m), "d_x", places, (WA, WB, *A, *B), [w(WA), w(WB), *map(full, (*A, *B))],
        jax.ShapeDtypeStruct((m * 2 * block, block), BF), pl.BlockSpec((2 * block, block), lambda i, s: (i, 0)), (m,), (),
        4 * m * block * block * (WA.shape[1] + WB.shape[1]) * 2 // 3)


def _merge(places, terms, up, down, one, three):
    n, h = one.shape[0], up.shape[0]
    one[...], three[...] = terms[:n], terms[n:2 * n]
    one[:h] = (terms[:h].astype(F32) + up[...].astype(F32)).astype(one.dtype)
    three[h:] = (terms[n + h:2 * n].astype(F32) + down[...].astype(F32)).astype(three.dtype)


def merge(terms, up, down):
    block = jax.ShapeDtypeStruct((2 * up.shape[0], up.shape[1]), terms.dtype)
    full = lambda v, rows=None: pl.BlockSpec((rows or v.shape[0], v.shape[1]), lambda i, s: (0, 0))
    return call(_merge, "merge", jnp.zeros(1, jnp.int32), (terms, up, down), [full(terms, 2 * block.shape[0]), full(up), full(down)],
                (block, block), (full(block), full(block)), (1,))


def per_device(tokens, cotangent, gate_weight, up_weight, down_weight):
    x, yh, yl, z, c = (lax.axis_index(n) for n in ("x", "yh", "yl", "z", "c"))
    rows, width = tokens.shape
    block = 2 * width
    home = c == yh
    first = yl == yh
    ints = lambda *v: jnp.stack(v).astype(jnp.int32)

    def trade(mine, other):
        return jnp.where(home, mine, other), jnp.where(home, other, mine)

    def chunk(lo, hi, *weights):
        gate, up, down = weights

        def part(e):
            return cat(cut(gate[:, lo:hi], e, 0), cut(up[:, lo:hi], e, 0), cut(down[lo:hi], e, 1).T, axis=1)

        return trade(part(c), sibling(part(1 - c)))

    def give_back(keep, got):
        mine, theirs = trade(keep, got)
        return ordered(c == 0, mine, sibling(theirs), 0)

    F = gate_weight.shape[1]
    split = SPLIT * F // 896
    weights = (gate_weight, up_weight, down_weight)
    half, pair = width, 2 * rows
    x_of = [(q - z) % 4 for q in range(4)]
    w_of = [(z + j) % 4 for j in range(4)]
    places = ints(*x_of, c)

    def total(term, up, down):
        return (term.astype(F32) + up.astype(F32) + down.astype(F32)).astype(BF)

    blocks = lambda flip: ints(*[q * 4 + ((p + yh + flip) % 2) * 2 + c for q in range(4) for p in range(2)])
    keepA, sendA = chunk(0, split, *weights)

    *weights, cotangent = after((*weights, cotangent), sendA)
    gotA = across(sendA)
    eighth = rows // 8
    part = columns(lax.dynamic_slice_in_dim(cotangent, (z * 2 + 1 - yl) * eighth, eighth, 0), blocks(1), width)
    part = behind(part)
    C = columns(cotangent, blocks(0), width, pair)
    keepB, sendB = chunk(split, F, *weights)
    ownA = cat(keepA, gotA)

    ownA, tokens, part, C, keepB, sendB = after((ownA, tokens, part, C, keepB, sendB))
    WA = lax.all_gather(ownA, "x", axis=0, tiled=True)
    near, off, opposite, part2 = beside(tokens), behind(tokens), across(tokens), beside(part)
    here = cat(ordered(first, tokens, near, 1), ordered(first, opposite, off, 1))
    part = ordered(yl == 0, part, part2, 0)

    here, part = after((here, part))
    z_before, z_after = ring(here, "z", 1), ring(here, "z", -1)
    c_before, c_after = ring(part, "z", 1), ring(part, "z", -1)

    z_before, z_after, c_before, c_after, sendB = after((z_before, z_after, c_before, c_after, sendB))
    up, down = ring(z_before[:rows], "z", 1), ring(z_after[rows:], "z", -1)
    c_up, c_down = ring(c_before[:eighth], "z", 1), ring(c_after[eighth:], "z", -1)
    ownB = cat(keepB, across(sendB))
    stack = cat(here, z_after, up, down, z_before)
    X = stack.reshape(4, pair, block)
    for j, v in enumerate((part, c_after, (c_up, c_down), c_before)):
        for i, v in enumerate(v if j == 2 else (v,)):
            C = lax.dynamic_update_slice_in_dim(C, v, rows + (z + j) % 4 * 2 * eighth + i * eighth, 0)

    ownB, stack, C = after((ownB, stack, C), WA)
    X = stack.reshape(4, pair, block)
    WB = lax.all_gather(ownB, "x", axis=0, tiled=True)

    def compute(W):
        theirs, mine = partial_x(X, W, places)
        theirs_d, mine_d = partial_c(C, W, ints(c))
        mine = activate(mine, sibling(theirs), mine_d, sibling(theirs_d), ints(c))
        other = sibling(mine)
        return mine, other, grads(X, C, mine, other, x_of, c, (0, 1, 2, 3))

    *A, termsA = compute(WA)
    sumA = lax.psum_scatter(termsA, "x", scatter_dimension=0, tiled=True)
    WB, X, C = after((WB, X, C), termsA)
    *B, termsB = compute(WB)
    sumB = lax.psum_scatter(termsB, "x", scatter_dimension=0, tiled=True)

    A, B = after((*A, *B), termsB)[:2], after((*A, *B), termsB)[2:]
    dx = d_x(WA, WB, A, B, w_of, c, (2, 1, 3, 0))
    up, down = ring(dx[:rows], "z", 1), ring(dx[rows:pair], "z", -1)
    terms = dx[pair:]
    one, three = merge(terms, up, down)
    up, down = ring(one, "z", 1), ring(three, "z", -1)
    dx = terms[2 * pair:].astype(F32) + up.astype(F32) + down.astype(F32)
    mine, theirs = jnp.where(first, dx[:, :width], dx[:, width:]), jnp.where(first, dx[:, width:], dx[:, :width]).astype(BF)
    gotA = across(sumA[half:])
    near, off, opposite = beside(theirs[:rows]), behind(theirs[rows:]), across(mine[rows:].astype(BF))
    d_tokens = mine[:rows] + near.astype(F32) + off.astype(F32) + opposite.astype(F32)
    sumA = give_back(sumA[:half], gotA)

    sumB, = after((sumB,), d_tokens, sumA)
    gotB = across(sumB[half:])
    sumB = give_back(sumB[:half], gotB)
    n, m = split, F - split
    gate, up, down = (cat(sumA[:, i * n:(i + 1) * n], sumB[:, i * m:(i + 1) * m], axis=1) for i in range(3))
    return d_tokens.astype(BF), gate, up, down.T


def solution(mesh):
    fine = Mesh(mesh.devices.reshape(4, 2, 2, 4, 2), ("z", "yl", "c", "x", "yh"))
    node, rep = ("x", "yh"), ("z", "yl", "c")
    return jax.shard_map(
        per_device,
        mesh=fine,
        in_specs=(P(node, rep), P(node, None), P(node, rep), P(node, rep), P(rep, node)),
        out_specs=(P(node, rep), P(node, rep), P(node, rep), P(rep, node)),
        check_vma=False,
    )
```

time: 782 us -> 342 us (0.44)
  waiting for transfers between devices: 692 us -> 128 us
  Pallas kernels: 0 us -> 91.6 us
  matrix products: 68.5 us -> 0 us
  starting transfers between devices: 0.27 us -> 47.9 us
  local copies, waits for them, and re-layouts: 5.55 us -> 40.5 us
  other arithmetic: 1.77 us -> 18.3 us
    reduce_scatter x3 -> x2, waiting for transfers between devices: 351 us -> 0.02 us  [the longest x1 0.02 us: per_device(): sumB = lax.psum_scatter(termsB, 'x', scatter_dimension=0, tiled=True)]
    all_gather x4 -> x2, waiting for transfers between devices: 338 us -> 12.3 us  [the longest x1 12.3 us: per_device(): WB = lax.all_gather(ownB, 'x', axis=0, tiled=True)]
    ppermute x0 -> x34, waiting for transfers between devices: none -> 116 us  [the longest x12 57.1 us: ring(): return lax.ppermute(v, axis, [(i, (i + step) % 4) for i in range(4)])]
    pallas_call x0 -> x12, Pallas kernels: none -> 91.6 us  [call(): pl.pallas_call(body, grid_spec=pltpu.PrefetchScalarGridSpec(num_scalar_pr...]
    dot_general x7 -> x0, matrix products: 68.5 us -> none  [the longest x1 13.3 us: per_device(): lax.dot_general(feats, both_grads, (((0,), (0,)), ((), ())), preferred_el...]
    ppermute x0 -> x34, starting transfers between devices: none -> 47.7 us  [the longest x12 17.6 us: ring(): return lax.ppermute(v, axis, [(i, (i + step) % 4) for i in range(4)])]
    slice x1 -> x22, local copies, waits for them, and re-layouts: 1.57 us -> 12.8 us  [the longest x1 3.76 us: per_device(): terms = dx[pair:]]
    unnamed x6 -> x37, local copies, waits for them, and re-layouts: 3.97 us -> 13.5 us
  transfers between devices with their start and end apart: 7 -> 38, of which waited for: 7 -> 23; matrix products, arithmetic and copies ran while one was open for 6% -> 11% of each run, Pallas kernels for 0% -> 27%
where the time goes in v1:
time: 342 us; the launch traced here: 341 us
  waiting for transfers between devices  128 us (37%)
  Pallas kernels  91.6 us (27%)
  starting transfers between devices  47.9 us (14%)
  local copies, waits for them, and re-layouts  40.5 us (12%)
  other arithmetic  18.3 us (5%)
  between operations  14.2 us (4%)
    pallas_call x12, Pallas kernels, call(): pl.pallas_call(body, grid_spec=pltpu.PrefetchScalarGridSpec(num_scalar_pr...  91.6 us
    ppermute x12, waiting for transfers between devices, ring(): return lax.ppermute(v, axis, [(i, (i + step) % 4) for i in range(4)])  57.1 us
    ppermute x6, waiting for transfers between devices, across(): return lax.ppermute(v, 'yh', SWAP)  29 us
    ppermute x12, starting transfers between devices, ring(): return lax.ppermute(v, axis, [(i, (i + step) % 4) for i in range(4)])  17.6 us
    ppermute x6, starting transfers between devices, across(): return lax.ppermute(v, 'yh', SWAP)  17.1 us
    unnamed x37, local copies, waits for them, and re-layouts  13.5 us
    ppermute x10, waiting for transfers between devices, sibling(): return lax.ppermute(v, 'c', SWAP)  13.2 us
    all_gather x1, waiting for transfers between devices, per_device(): WB = lax.all_gather(ownB, 'x', axis=0, tiled=True)  12.3 us
  transfers between devices with their start and end apart: 38, of which 23 were waited for; matrix products, arithmetic and copies ran while one was open for 11% of the time, Pallas kernels for 27%

profile of v1, /device:TPU:1, one launch (start us, length us, event | category | flops | bytes accessed | tf_op | source)
XLA Modules:
  0.0 340.5 jit_solution(10023922901953388392)
XLA Ops:
  21.0 3.0 collective-permute-start.1
  24.0 6.4 %columns.3 = bf16[1024,2048]{1,0:T(8,128)(2,1)} custom-call(s32[8]{0:T(128)} %stack.117.places, bf16[512,4096]{1,0:T(8,128)(2,1)} %src), custom_call_target="tpu_custom_call" | custom-call | bytes 83886 | tf_op jit(solution)/shard_map/columns/pallas_call | solution.py:60
  32.3 5.0 %columns.2 = bf16[64,2048]{1,0:T(8,128)(2,1)} custom-call(s32[8]{0:T(128)} %stack.112.places, bf16[64,4096]{1,0:T(8,128)(2,1)} %constant_dynamic-slice_fusion.4.src), custom_call_target="tpu_custom_call" | custom-call | bytes 7864 | tf_op jit(solution)/shard_map/columns/pallas_call | solution.py:60
  42.9 4.6 %collective-permute-done.2 = bf16[64,2048]{1,0:T(8,128)(2,1)S(1)} collective-permute-done((bf16[64,2048]{1,0:T(8,128)(2,1)}, bf16[64,2048]{1,0:T(8,128)(2,1)S(1)}, u32[]{:S(2)}, u32[]{:S(2)}) %collective-permute-start.2) | collective-permute-done | bytes 262176 | tf_op jit(solution)/shard_map/ppermute | solution.py:34
  51.8 3.2 collective-permute-done.4
  55.0 8.3 %collective-permute-done.5 = bf16[512,256]{1,0:T(8,128)(2,1)S(1)} collective-permute-done((bf16[512,256]{1,0:T(8,128)(2,1)S(1)}, bf16[512,256]{1,0:T(8,128)(2,1)S(1)}, u32[]{:S(2)}, u32[]{:S(2)}) %collective-permute-start.5) | collective-permute-done | bytes 262176 | tf_op jit(solution)/shard_map/ppermute | solution.py:26
  71.1 2.7 collective-permute-start.11
  76.8 27.8 %collective-permute-done.10 = bf16[128,2048]{1,0:T(8,128)(2,1)} collective-permute-done((bf16[128,2048]{1,0:T(8,128)(2,1)}, bf16[128,2048]{1,0:T(8,128)(2,1)}, u32[]{:S(2)}, u32[]{:S(2)}) %collective-permute-start.10) | collective-permute-done | bytes 524320 | tf_op jit(solution)/shard_map/ppermute | solution.py:18
  113.3 3.2 collective-permute-start.12
  129.0 9.2 %partial_x.2 = (bf16[512,1024]{1,0:T(8,128)(2,1)}, f32[512,1024]{1,0:T(8,128)}) custom-call(s32[5]{0:T(128)} %stack.123.places, bf16[4,1024,512]{2,1,0:T(8,128)(2,1)} %bitcast.21.x0.x1.x2.x3.xm.xo, bf16[4,1024,512]{2,1,0:T(8,128)(2,1)} %bitcast.21.x0.x1.x2.x3.xm.xo, bf16[4,1024,512]{2,1,0:T(8,128)(2,1)} %bitcast.21.x0.x1.x2.x3.xm.xo, ...), custom_call_target="tpu_custom_call" | custom-call | flops 64424508 | bytes 262144 | tf_op jit(solution)/shard_map/partial_x/pallas_call | solution.py:60
  138.3 3.7 %collective-permute-start.17 = (bf16[512,1024]{1,0:T(8,128)(2,1)}, bf16[512,1024]{1,0:T(8,128)(2,1)S(1)}, u32[]{:S(2)}, u32[]{:S(2)}) collective-permute-start(bf16[512,1024]{1,0:T(8,128)(2,1)} %get-tuple-element.63), channel_id=1, source_target_pairs={{0,8},{8,0},{1,9},{9,1},{2,10},{10,2},{3,11},{11,3},{4,12},{12,4},... | collective-permute-start | bytes 3145736 | tf_op jit(solution)/shard_map/ppermute | solution.py:22
  142.0 6.5 %partial_c.2 = (bf16[512,512]{1,0:T(8,128)(2,1)}, f32[512,512]{1,0:T(8,128)}) custom-call(s32[1]{0:T(128)} %bitcast.4.places, bf16[1024,2048]{1,0:T(8,128)(2,1)} %constant_dynamic-update-slice_fusion.5.cot.cm.co, bf16[2048,1536]{1,0:T(8,128)(2,1)} %all-gather.3.cloned.1.call-done.w.wa), custom_call_target="tpu_custom_call" | custom-call | flops 21474836 | bytes 120586 | tf_op jit(solution)/shard_map/partial_c/pallas_call | solution.py:60
  151.7 4.4 %activate.2.dm.ma = bf16[512,1536]{1,0:T(8,128)(2,1)} custom-call(s32[1]{0:T(128)} %bitcast.4.places, f32[512,1024]{1,0:T(8,128)} %get-tuple-element.62.mine, bf16[512,1024]{1,0:T(8,128)(2,1)} %copy-done.5, f32[512,512]{1,0:T(8,128)} %get-tuple-element.64.mine_d, bf16[512,512]{1,0:T(8,128)(2,1)} %copy-done.11), custom_call_target="tpu_custom_call" | custom-call | flops 78643 | bytes 62914 | tf_op jit(solution)/shard_map/activate/pallas_call | solution.py:60
  157.0 2.8 collective-permute-done.19.do.oa
  161.0 12.3 %grads.2 = bf16[2048,1536]{1,0:T(8,128)(2,1)} custom-call(s32[9]{0:T(128)} %stack.122.places, bf16[4,1024,512]{2,1,0:T(8,128)(2,1)} %bitcast.21.x0.x1.x2.x3.xm.xo, bf16[4,1024,512]{2,1,0:T(8,128)(2,1)} %bitcast.21.x0.x1.x2.x3.xm.xo, bf16[1024,2048]{1,0:T(8,128)(2,1)} %constant_dynamic-update-slice_fusion.5.cot.cm.co, ...), custom_call_target="tpu_custom_call" | custom-call | flops 64424508 | bytes 262144 | tf_op jit(solution)/shard_map/grads/pallas_call | solution.py:60
  173.4 12.3 %all-gather.5.cloned.1.call-done.w.wb = bf16[2048,1152]{1,0:T(8,128)(2,1)} async-done(((bf16[512,1152]{1,0:T(8,128)(2,1)}), bf16[2048,1152]{1,0:T(8,128)(2,1)}) %all-gather.5.cloned.1.call-update) | async-done | bytes 4718608 | tf_op jit(solution)/shard_map/all_gather | solution.py:257
  185.7 8.9 %partial_x.3 = (bf16[512,768]{1,0:T(8,128)(2,1)}, f32[512,768]{1,0:T(8,128)}) custom-call(s32[5]{0:T(128)} %stack.123.places, bf16[4,1024,512]{2,1,0:T(8,128)(2,1)} %bitcast.21.x0.x1.x2.x3.xm.xo, bf16[4,1024,512]{2,1,0:T(8,128)(2,1)} %bitcast.21.x0.x1.x2.x3.xm.xo, bf16[4,1024,512]{2,1,0:T(8,128)(2,1)} %bitcast.21.x0.x1.x2.x3.xm.xo, ...), custom_call_target="tpu_custom_call" | custom-call | flops 48318384 | bytes 238551 | tf_op jit(solution)/shard_map/partial_x/pallas_call | solution.py:60
  195.3 6.4 %partial_c.3 = (bf16[512,384]{1,0:T(8,128)(2,1)}, f32[512,384]{1,0:T(8,128)}) custom-call(s32[1]{0:T(128)} %bitcast.4.places, bf16[1024,2048]{1,0:T(8,128)(2,1)} %constant_dynamic-update-slice_fusion.5.cot.cm.co, bf16[2048,1152]{1,0:T(8,128)(2,1)} %all-gather.5.cloned.1.call-done.w.wb), custom_call_target="tpu_custom_call" | custom-call | flops 16106127 | bytes 100925 | tf_op jit(solution)/shard_map/partial_c/pallas_call | solution.py:60
  204.7 4.1 %activate.3.dm.mb = bf16[512,1152]{1,0:T(8,128)(2,1)} custom-call(s32[1]{0:T(128)} %bitcast.4.places, f32[512,768]{1,0:T(8,128)} %get-tuple-element.68.mine, bf16[512,768]{1,0:T(8,128)(2,1)} %copy-done.6, f32[512,384]{1,0:T(8,128)} %get-tuple-element.71.mine_d, bf16[512,384]{1,0:T(8,128)(2,1)} %copy-done.13), custom_call_target="tpu_custom_call" | custom-call | flops 58982 | bytes 47185 | tf_op jit(solution)/shard_map/activate/pallas_call | solution.py:60
  209.0 2.9 collective-permute-done.22.do.ob
  212.9 11.1 %grads.3 = bf16[2048,1152]{1,0:T(8,128)(2,1)} custom-call(s32[9]{0:T(128)} %stack.122.places, bf16[4,1024,512]{2,1,0:T(8,128)(2,1)} %bitcast.21.x0.x1.x2.x3.xm.xo, bf16[4,1024,512]{2,1,0:T(8,128)(2,1)} %bitcast.21.x0.x1.x2.x3.xm.xo, bf16[1024,2048]{1,0:T(8,128)(2,1)} %constant_dynamic-update-slice_fusion.5.cot.cm.co, ...), custom_call_target="tpu_custom_call" | custom-call | flops 48318384 | bytes 238551 | tf_op jit(solution)/shard_map/grads/pallas_call | solution.py:60
  224.6 13.7 %d_x.1 = bf16[4096,512]{1,0:T(8,128)(2,1)} custom-call(s32[5]{0:T(128)} %stack.103.places, bf16[2048,1536]{1,0:T(8,128)(2,1)} %all-gather.3.cloned.1.call-done.w.wa, bf16[2048,1152]{1,0:T(8,128)(2,1)} %all-gather.5.cloned.1.call-done.w.wb, bf16[512,1536]{1,0:T(8,128)(2,1)} %activate.2.dm.ma, bf16[512,1536]{1,0:T(8,128)(2,1)} %copy-done, ...), custom_call_target="tpu_custom_call" | custom-call | flops 75161928 | bytes 207093 | tf_op jit(solution)/shard_map/d_x/pallas_call | solution.py:60
  242.3 3.8 %slice.132.terms = bf16[3072,512]{1,0:T(8,128)(2,1)} slice(bf16[4096,512]{1,0:T(8,128)(2,1)} %d_x.1), slice={[1024:4096], [0:512]} | slice | bytes 6291456 | tf_op jit(solution)/shard_map/slice | solution.py:275
  246.1 8.2 %collective-permute-done.23.up = bf16[512,512]{1,0:T(8,128)(2,1)S(1)} collective-permute-done((bf16[512,512]{1,0:T(8,128)(2,1)S(1)}, bf16[512,512]{1,0:T(8,128)(2,1)S(1)}, u32[]{:S(2)}, u32[]{:S(2)}) %collective-permute-start.23) | collective-permute-done | bytes 524320 | tf_op jit(solution)/shard_map/ppermute | solution.py:18
  255.8 3.4 merge.1
  263.1 2.8 collective-permute-start.30
  265.9 18.6 %collective-permute-done.25 = bf16[1024,512]{1,0:T(8,128)(2,1)S(1)} collective-permute-done((bf16[1024,512]{1,0:T(8,128)(2,1)}, bf16[1024,512]{1,0:T(8,128)(2,1)S(1)}, u32[]{:S(2)}, u32[]{:S(2)}) %collective-permute-start.25) | collective-permute-done | bytes 1048608 | tf_op jit(solution)/shard_map/ppermute | solution.py:18
  289.6 2.8 collective-permute-start.29
  294.1 5.1 %collective-permute-done.29 = bf16[512,256]{1,0:T(8,128)(2,1)} collective-permute-done((bf16[512,256]{1,0:T(8,128)(2,1)S(1)}, bf16[512,256]{1,0:T(8,128)(2,1)}, u32[]{:S(2)}, u32[]{:S(2)}) %collective-permute-start.29) | collective-permute-done | bytes 262176 | tf_op jit(solution)/shard_map/ppermute | solution.py:26
  299.2 5.6 %collective-permute-done.27 = bf16[512,256]{1,0:T(8,128)(2,1)S(1)} collective-permute-done((bf16[512,256]{1,0:T(8,128)(2,1)}, bf16[512,256]{1,0:T(8,128)(2,1)S(1)}, u32[]{:S(2)}, u32[]{:S(2)}) %collective-permute-start.27) | collective-permute-done | bytes 262176 | tf_op jit(solution)/shard_map/ppermute | solution.py:30
  309.9 2.8 collective-permute-start.32
  312.6 13.2 %collective-permute-done.32 = bf16[256,1152]{1,0:T(8,128)(2,1)S(1)} collective-permute-done((bf16[256,1152]{1,0:T(8,128)(2,1)S(1)}, bf16[256,1152]{1,0:T(8,128)(2,1)S(1)}, u32[]{:S(2)}, u32[]{:S(2)}) %collective-permute-start.32) | collective-permute-done | bytes 589856 | tf_op jit(solution)/shard_map/ppermute | solution.py:26
  (158 shorter events, 97.6 us)
Async XLA Ops:
  7.2 121.1 %all-gather.3.cloned.1.call-start = ((), (), s32[]{:S(2)}) async-start(), calls=%async_computation.2 | async-start | bytes 7864320 | tf_op jit(solution)/shard_map/all_gather | solution.py:236
  19.3 18.8 %collective-permute-start.3 = (bf16[256,1152]{1,0:T(8,128)(2,1)}, bf16[256,1152]{1,0:T(8,128)(2,1)S(1)}, u32[]{:S(2)}, u32[]{:S(2)}) collective-permute-start(bf16[256,1152]{1,0:T(8,128)(2,1)} %pad_maximum_fusion.8), channel_id=1, source_target_pairs={{0,8},{8,0},{1,9},{9,1},{2,10},{10,2},{3,11},{11,3},{4,12},{12,4},... | collective-permute-start | bytes 1769480 | tf_op jit(solution)/shard_map/ppermute | solution.py:22
  21.0 20.6 %collective-permute-start.1 = (bf16[256,1536]{1,0:T(8,128)(2,1)S(1)}, bf16[256,1536]{1,0:T(8,128)(2,1)S(1)}, u32[]{:S(2)}, u32[]{:S(2)}) collective-permute-start(bf16[256,1536]{1,0:T(8,128)(2,1)S(1)} %copy-done.7), channel_id=1, source_target_pairs={{0,1},{1,0},{2,3},{3,2},{4,5},{5,4},{6,7},{7,6},{8,9},{9,8},{10,11... | collective-permute-start | bytes 2359304 | tf_op jit(solution)/shard_map/ppermute | solution.py:26
  37.2 10.2 %collective-permute-start.2 = (bf16[64,2048]{1,0:T(8,128)(2,1)}, bf16[64,2048]{1,0:T(8,128)(2,1)S(1)}, u32[]{:S(2)}, u32[]{:S(2)}) collective-permute-start(bf16[64,2048]{1,0:T(8,128)(2,1)} %columns.2), channel_id=1, source_target_pairs={{0,17},{17,0},{1,16},{16,1},{2,19},{19,2},{3,18},{18,3},{4,21},{21... | collective-permute-start | bytes 786440 | tf_op jit(solution)/shard_map/ppermute | solution.py:34
  47.5 138.2 %all-gather.5.cloned.1.call-start = ((), (), s32[]{:S(2)}) async-start(), calls=%async_computation.3 | async-start | bytes 5898240 | tf_op jit(solution)/shard_map/all_gather | solution.py:257
  47.6 7.4 %collective-permute-start.4 = (bf16[512,256]{1,0:T(8,128)(2,1)S(1)}, bf16[512,256]{1,0:T(8,128)(2,1)S(1)}, u32[]{:S(2)}, u32[]{:S(2)}) collective-permute-start(bf16[512,256]{1,0:T(8,128)(2,1)S(1)} %copy-done.14), channel_id=1, source_target_pairs={{0,16},{16,0},{1,17},{17,1},{2,18},{18,2},{3,19},{19,3},{4,20},{20... | collective-permute-start | bytes 786440 | tf_op jit(solution)/shard_map/ppermute | solution.py:30
  49.1 14.2 %collective-permute-start.5 = (bf16[512,256]{1,0:T(8,128)(2,1)S(1)}, bf16[512,256]{1,0:T(8,128)(2,1)S(1)}, u32[]{:S(2)}, u32[]{:S(2)}) collective-permute-start(bf16[512,256]{1,0:T(8,128)(2,1)S(1)} %copy-done.14), channel_id=1, source_target_pairs={{0,1},{1,0},{2,3},{3,2},{4,5},{5,4},{6,7},{7,6},{8,9},{9,8},{10,11... | collective-permute-start | bytes 786440 | tf_op jit(solution)/shard_map/ppermute | solution.py:26
  51.7 13.6 %collective-permute-start.6 = (bf16[512,256]{1,0:T(8,128)(2,1)S(1)}, bf16[512,256]{1,0:T(8,128)(2,1)S(1)}, u32[]{:S(2)}, u32[]{:S(2)}) collective-permute-start(bf16[512,256]{1,0:T(8,128)(2,1)S(1)} %copy-done.14), channel_id=1, source_target_pairs={{0,17},{17,0},{1,16},{16,1},{2,19},{19,2},{3,18},{18,3},{4,21},{21... | collective-permute-start | bytes 786440 | tf_op jit(solution)/shard_map/ppermute | solution.py:34
  51.7 14.6 %collective-permute-start.7 = (bf16[64,2048]{1,0:T(8,128)(2,1)S(1)}, bf16[64,2048]{1,0:T(8,128)(2,1)S(1)}, u32[]{:S(2)}, u32[]{:S(2)}) collective-permute-start(bf16[64,2048]{1,0:T(8,128)(2,1)S(1)} %collective-permute-done.2), channel_id=1, source_target_pairs={{0,16},{16,0},{1,17},{17,1},{2,18},{18,2},{3,19},{19,3},{4,20},{20... | collective-permute-start | bytes 786440 | tf_op jit(solution)/shard_map/ppermute | solution.py:30
  67.2 37.4 %collective-permute-start.8 = (bf16[1024,512]{1,0:T(8,128)(2,1)S(1)}, bf16[1024,512]{1,0:T(8,128)(2,1)S(1)}, u32[]{:S(2)}, u32[]{:S(2)}) collective-permute-start(bf16[1024,512]{1,0:T(8,128)(2,1)S(1)} %pad_maximum_fusion.2), channel_id=1, source_target_pairs={{0,32},{32,64},{64,96},{96,0},{1,33},{33,65},{65,97},{97,1},{2,34}... | collective-permute-start | bytes 3145736 | tf_op jit(solution)/shard_map/ppermute | solution.py:18
  69.0 35.6 %collective-permute-start.9 = (bf16[1024,512]{1,0:T(8,128)(2,1)S(1)}, bf16[1024,512]{1,0:T(8,128)(2,1)S(1)}, u32[]{:S(2)}, u32[]{:S(2)}) collective-permute-start(bf16[1024,512]{1,0:T(8,128)(2,1)S(1)} %pad_maximum_fusion.2), channel_id=1, source_target_pairs={{0,96},{32,0},{64,32},{96,64},{1,97},{33,1},{65,33},{97,65},{2,98}... | collective-permute-start | bytes 3145736 | tf_op jit(solution)/shard_map/ppermute | solution.py:18
  71.1 33.5 %collective-permute-start.10 = (bf16[128,2048]{1,0:T(8,128)(2,1)}, bf16[128,2048]{1,0:T(8,128)(2,1)}, u32[]{:S(2)}, u32[]{:S(2)}) collective-permute-start(bf16[128,2048]{1,0:T(8,128)(2,1)} %maximum_select_fusion.4), channel_id=1, source_target_pairs={{0,32},{32,64},{64,96},{96,0},{1,33},{33,65},{65,97},{97,1},{2,34}... | collective-permute-start | bytes 1572872 | tf_op jit(solution)/shard_map/ppermute | solution.py:18
  71.1 33.5 %collective-permute-start.11 = (bf16[128,2048]{1,0:T(8,128)(2,1)}, bf16[128,2048]{1,0:T(8,128)(2,1)}, u32[]{:S(2)}, u32[]{:S(2)}) collective-permute-start(bf16[128,2048]{1,0:T(8,128)(2,1)} %maximum_select_fusion.4), channel_id=1, source_target_pairs={{0,96},{32,0},{64,32},{96,64},{1,97},{33,1},{65,33},{97,65},{2,98}... | collective-permute-start | bytes 1572872 | tf_op jit(solution)/shard_map/ppermute | solution.py:18
  105.6 12.8 %collective-permute-start.15 = (bf16[64,2048]{1,0:T(8,128)(2,1)S(1)}, bf16[64,2048]{1,0:T(8,128)(2,1)S(1)}, u32[]{:S(2)}, u32[]{:S(2)}) collective-permute-start(bf16[64,2048]{1,0:T(8,128)(2,1)S(1)} %slice.108), channel_id=1, source_target_pairs={{0,32},{32,64},{64,96},{96,0},{1,33},{33,65},{65,97},{97,1},{2,34}... | collective-permute-start | bytes 786440 | tf_op jit(solution)/shard_map/ppermute | solution.py:18
  108.2 11.0 %collective-permute-start.16 = (bf16[64,2048]{1,0:T(8,128)(2,1)S(1)}, bf16[64,2048]{1,0:T(8,128)(2,1)S(1)}, u32[]{:S(2)}, u32[]{:S(2)}) collective-permute-start(bf16[64,2048]{1,0:T(8,128)(2,1)S(1)} %slice.109), channel_id=1, source_target_pairs={{0,96},{32,0},{64,32},{96,64},{1,97},{33,1},{65,33},{97,65},{2,98}... | collective-permute-start | bytes 786440 | tf_op jit(solution)/shard_map/ppermute | solution.py:18
  110.6 13.5 %collective-permute-start.13 = (bf16[512,512]{1,0:T(8,128)(2,1)S(1)}, bf16[512,512]{1,0:T(8,128)(2,1)S(1)}, u32[]{:S(2)}, u32[]{:S(2)}) collective-permute-start(bf16[512,512]{1,0:T(8,128)(2,1)S(1)} %slice.106), channel_id=1, source_target_pairs={{0,32},{32,64},{64,96},{96,0},{1,33},{33,65},{65,97},{97,1},{2,34}... | collective-permute-start | bytes 1572872 | tf_op jit(solution)/shard_map/ppermute | solution.py:18
  110.6 14.5 %collective-permute-start.14 = (bf16[512,512]{1,0:T(8,128)(2,1)S(1)}, bf16[512,512]{1,0:T(8,128)(2,1)S(1)}, u32[]{:S(2)}, u32[]{:S(2)}) collective-permute-start(bf16[512,512]{1,0:T(8,128)(2,1)S(1)} %slice.107), channel_id=1, source_target_pairs={{0,96},{32,0},{64,32},{96,64},{1,97},{33,1},{65,33},{97,65},{2,98}... | collective-permute-start | bytes 1572872 | tf_op jit(solution)/shard_map/ppermute | solution.py:18
  113.3 13.8 %collective-permute-start.12 = (bf16[256,1152]{1,0:T(8,128)(2,1)S(1)}, bf16[256,1152]{1,0:T(8,128)(2,1)S(1)}, u32[]{:S(2)}, u32[]{:S(2)}) collective-permute-start(bf16[256,1152]{1,0:T(8,128)(2,1)S(1)} %copy-done.9), channel_id=1, source_target_pairs={{0,1},{1,0},{2,3},{3,2},{4,5},{5,4},{6,7},{7,6},{8,9},{9,8},{10,11... | collective-permute-start | bytes 1769480 | tf_op jit(solution)/shard_map/ppermute | solution.py:26
  128.3 133.6 %reduce-scatter.3.cloned.1.call-start = ((), (), s32[]{:S(2)}) async-start(), calls=%async_computation.4 | async-start | bytes 7864320 | tf_op jit(solution)/shard_map/reduce_scatter | solution.py:267
  138.3 12.3 %collective-permute-start.17 = (bf16[512,1024]{1,0:T(8,128)(2,1)}, bf16[512,1024]{1,0:T(8,128)(2,1)S(1)}, u32[]{:S(2)}, u32[]{:S(2)}) collective-permute-start(bf16[512,1024]{1,0:T(8,128)(2,1)} %get-tuple-element.63), channel_id=1, source_target_pairs={{0,8},{8,0},{1,9},{9,1},{2,10},{10,2},{3,11},{11,3},{4,12},{12,4},... | collective-permute-start | bytes 3145736 | tf_op jit(solution)/shard_map/ppermute | solution.py:22
  173.3 135.4 %reduce-scatter.5.cloned.1.call-start = ((), (), s32[]{:S(2)}) async-start(), calls=%async_computation.5 | async-start | bytes 5898240 | tf_op jit(solution)/shard_map/reduce_scatter | solution.py:270
  194.7 9.0 %collective-permute-start.20 = (bf16[512,768]{1,0:T(8,128)(2,1)}, bf16[512,768]{1,0:T(8,128)(2,1)S(1)}, u32[]{:S(2)}, u32[]{:S(2)}) collective-permute-start(bf16[512,768]{1,0:T(8,128)(2,1)} %get-tuple-element.69), channel_id=1, source_target_pairs={{0,8},{8,0},{1,9},{9,1},{2,10},{10,2},{3,11},{11,3},{4,12},{12,4},... | collective-permute-start | bytes 2359304 | tf_op jit(solution)/shard_map/ppermute | solution.py:22
  239.6 14.7 %collective-permute-start.23 = (bf16[512,512]{1,0:T(8,128)(2,1)S(1)}, bf16[512,512]{1,0:T(8,128)(2,1)S(1)}, u32[]{:S(2)}, u32[]{:S(2)}) collective-permute-start(bf16[512,512]{1,0:T(8,128)(2,1)S(1)} %get-tuple-element.85), channel_id=1, source_target_pairs={{0,32},{32,64},{64,96},{96,0},{1,33},{33,65},{65,97},{97,1},{2,34}... | collective-permute-start | bytes 1572872 | tf_op jit(solution)/shard_map/ppermute | solution.py:18
  240.7 13.5 %collective-permute-start.24 = (bf16[512,512]{1,0:T(8,128)(2,1)S(1)}, bf16[512,512]{1,0:T(8,128)(2,1)S(1)}, u32[]{:S(2)}, u32[]{:S(2)}) collective-permute-start(bf16[512,512]{1,0:T(8,128)(2,1)S(1)} %get-tuple-element.84), channel_id=1, source_target_pairs={{0,96},{32,0},{64,32},{96,64},{1,97},{33,1},{65,33},{97,65},{2,98}... | collective-permute-start | bytes 1572872 | tf_op jit(solution)/shard_map/ppermute | solution.py:18
  259.2 25.2 %collective-permute-start.25 = (bf16[1024,512]{1,0:T(8,128)(2,1)}, bf16[1024,512]{1,0:T(8,128)(2,1)S(1)}, u32[]{:S(2)}, u32[]{:S(2)}) collective-permute-start(bf16[1024,512]{1,0:T(8,128)(2,1)} %get-tuple-element.77), channel_id=1, source_target_pairs={{0,32},{32,64},{64,96},{96,0},{1,33},{33,65},{65,97},{97,1},{2,34}... | collective-permute-start | bytes 3145736 | tf_op jit(solution)/shard_map/ppermute | solution.py:18
  259.4 25.1 %collective-permute-start.26 = (bf16[1024,512]{1,0:T(8,128)(2,1)}, bf16[1024,512]{1,0:T(8,128)(2,1)S(1)}, u32[]{:S(2)}, u32[]{:S(2)}) collective-permute-start(bf16[1024,512]{1,0:T(8,128)(2,1)} %get-tuple-element.78), channel_id=1, source_target_pairs={{0,96},{32,0},{64,32},{96,64},{1,97},{33,1},{65,33},{97,65},{2,98}... | collective-permute-start | bytes 3145736 | tf_op jit(solution)/shard_map/ppermute | solution.py:18
  263.1 23.2 %collective-permute-start.30 = (bf16[256,1536]{1,0:T(8,128)(2,1)S(1)}, bf16[256,1536]{1,0:T(8,128)(2,1)S(1)}, u32[]{:S(2)}, u32[]{:S(2)}) collective-permute-start(bf16[256,1536]{1,0:T(8,128)(2,1)S(1)} %slice.142), channel_id=1, source_target_pairs={{0,1},{1,0},{2,3},{3,2},{4,5},{5,4},{6,7},{7,6},{8,9},{9,8},{10,11... | collective-permute-start | bytes 2359304 | tf_op jit(solution)/shard_map/ppermute | solution.py:26
  287.7 19.1 %collective-permute-start.31 = (bf16[256,1536]{1,0:T(8,128)(2,1)S(1)}, bf16[256,1536]{1,0:T(8,128)(2,1)}, u32[]{:S(2)}, u32[]{:S(2)}) collective-permute-start(bf16[256,1536]{1,0:T(8,128)(2,1)S(1)} %get-tuple-element.87), channel_id=1, source_target_pairs={{0,8},{8,0},{1,9},{9,1},{2,10},{10,2},{3,11},{11,3},{4,12},{12,4},... | collective-permute-start | bytes 2359304 | tf_op jit(solution)/shard_map/ppermute | solution.py:22
  289.6 9.6 %collective-permute-start.29 = (bf16[512,256]{1,0:T(8,128)(2,1)S(1)}, bf16[512,256]{1,0:T(8,128)(2,1)}, u32[]{:S(2)}, u32[]{:S(2)}) collective-permute-start(bf16[512,256]{1,0:T(8,128)(2,1)S(1)} %slice.164), channel_id=1, source_target_pairs={{0,1},{1,0},{2,3},{3,2},{4,5},{5,4},{6,7},{7,6},{8,9},{9,8},{10,11... | collective-permute-start | bytes 786440 | tf_op jit(solution)/shard_map/ppermute | solution.py:26
  293.2 11.6 %collective-permute-start.27 = (bf16[512,256]{1,0:T(8,128)(2,1)}, bf16[512,256]{1,0:T(8,128)(2,1)S(1)}, u32[]{:S(2)}, u32[]{:S(2)}) collective-permute-start(bf16[512,256]{1,0:T(8,128)(2,1)} %get-tuple-element.100), channel_id=1, source_target_pairs={{0,16},{16,0},{1,17},{17,1},{2,18},{18,2},{3,19},{19,3},{4,20},{20... | collective-permute-start | bytes 786440 | tf_op jit(solution)/shard_map/ppermute | solution.py:30
  293.5 11.5 %collective-permute-start.28 = (bf16[512,256]{1,0:T(8,128)(2,1)}, bf16[512,256]{1,0:T(8,128)(2,1)S(1)}, u32[]{:S(2)}, u32[]{:S(2)}) collective-permute-start(bf16[512,256]{1,0:T(8,128)(2,1)} %get-tuple-element.101), channel_id=1, source_target_pairs={{0,17},{17,0},{1,16},{16,1},{2,19},{19,2},{3,18},{18,3},{4,21},{21... | collective-permute-start | bytes 786440 | tf_op jit(solution)/shard_map/ppermute | solution.py:34
  309.9 15.9 %collective-permute-start.32 = (bf16[256,1152]{1,0:T(8,128)(2,1)S(1)}, bf16[256,1152]{1,0:T(8,128)(2,1)S(1)}, u32[]{:S(2)}, u32[]{:S(2)}) collective-permute-start(bf16[256,1152]{1,0:T(8,128)(2,1)S(1)} %slice.124), channel_id=1, source_target_pairs={{0,1},{1,0},{2,3},{3,2},{4,5},{5,4},{6,7},{7,6},{8,9},{9,8},{10,11... | collective-permute-start | bytes 1769480 | tf_op jit(solution)/shard_map/ppermute | solution.py:26
  (25 other events, 56.3 us)
Sparse Core Ops, SparseCore 0:
  47.6 67.9 all-gather.2
  128.4 57.2 all-gather.4
  188.1 64.3 reduce-scatter.2
  254.8 50.7 reduce-scatter.4

commit v2 on v1

--- a/solution.py
+++ b/solution.py
@@ -69,13 +69,15 @@
 
 
 def _copy(places, src, dst):
-    dst[...] = src[...]
-
-
-def columns(v, places, width, height=None):
-    rows, n = v.shape[0], places.shape[0]
-    return call(_copy, "columns", places, (v,), [pl.BlockSpec((rows, width), lambda i, s: (0, s[i]))],
-                jax.ShapeDtypeStruct((height or rows, n * width), v.dtype), pl.BlockSpec((rows, width), lambda i, s: (0, i)), (n,))
+    dst[0] = src[...]
+
+
+def columns(v, places, width, row, rows, height):
+    n = places.shape[0]
+    places = jnp.concatenate([places, jnp.stack([row]).astype(jnp.int32)])
+    return call(_copy, "columns", places, (v,), [pl.BlockSpec((rows, width), lambda i, s: (s[n], s[i]))],
+                jax.ShapeDtypeStruct((n // 2, height, 2 * width), v.dtype),
+                pl.BlockSpec((1, rows, width), lambda i, s: (i // 2, 0, i % 2)), (n,))
 
 
 def _partial_x(places, x0, x1, x2, x3, w, theirs, mine):
@@ -100,7 +102,8 @@
 def _partial_c(places, cot, w, theirs, mine):
     block = theirs.shape[0]
     for out, half in ((theirs, 1 - places[0]), (mine, places[0])):
-        out[...] = mm(cot[pl.ds(pl.multiple_of(half * block, block), block)], w[...]).astype(out.dtype)
+        at = pl.ds(pl.multiple_of(half * block, block), block)
+        out[...] = sum(mm(cot[k, at], w[k * block:(k + 1) * block]) for k in range(4)).astype(out.dtype)
 
 
 def partial_c(C, W, places):
@@ -109,7 +112,7 @@
     step = n // 2 if n % 512 == 0 else n
     return call(
         _partial_c, "partial_c", places, (C, W),
-        [pl.BlockSpec(C.shape, lambda i, s: (0, 0)), pl.BlockSpec((depth, step), lambda i, s: (0, 2 * (n // step) + i))],
+        [pl.BlockSpec(C.shape, lambda i, s: (0, 0, 0)), pl.BlockSpec((depth, step), lambda i, s: (0, 2 * (n // step) + i))],
         (jax.ShapeDtypeStruct((block, n), BF), jax.ShapeDtypeStruct((block, n), F32)),
         (pl.BlockSpec((block, step), lambda i, s: (0, i)),) * 2, (n // step,), (), 16 * block * block * n)
 
@@ -133,22 +136,27 @@
                 jax.ShapeDtypeStruct((rows, 3 * n), BF), spec(3 * n), (4,), (), 30 * rows * n)
 
 
-def _grads(n, places, xm, xo, cm, co, dm, do, out):
-    out[:, :2 * n] = (mm(xm[0], dm[:, :2 * n], 0, 0) + mm(xo[0], do[:, :2 * n], 0, 0)).astype(out.dtype)
-    out[:, 2 * n:] = (mm(cm[...], dm[:, 2 * n:], 0, 0) + mm(co[...], do[:, 2 * n:], 0, 0)).astype(out.dtype)
-
-
-def grads(X, C, mine, other, x_of, c, ks):
+def _grads(n, m, places, xm, xo, cm, co, dm, do, out):
+    half = out.shape[0] // 2
+    gate_up = (mm(xm[0], dm[:, :2 * n], 0, 0) + mm(xo[0], do[:, :2 * n], 0, 0)).astype(out.dtype)
+    down = (mm(cm[0], dm[:, 2 * n:], 0, 0) + mm(co[0], do[:, 2 * n:], 0, 0)).astype(out.dtype)
+    for i in range(2):
+        at = pl.ds(pl.multiple_of((i + places[2 * m + 1]) % 2 * half, half), half)
+        out[at, :2 * n] = gate_up[i * half:(i + 1) * half]
+        out[at, 2 * n:] = down[i * half:(i + 1) * half]
+
+
+def grads(X, C, mine, other, x_of, c, ks, turned=0):
     block, n3 = mine.shape
     m = len(ks)
-    places = jnp.stack([*(x_of[k] for k in ks), *ks, c]).astype(jnp.int32)
+    places = jnp.stack([*(x_of[k] for k in ks), *ks, c, turned]).astype(jnp.int32)
     full = pl.BlockSpec((block, n3), lambda i, s: (0, 0))
     return call(
-        functools.partial(_grads, n3 // 3), "grads", places, (X, X, C, C, mine, other),
+        functools.partial(_grads, n3 // 3, m), "grads", places, (X, X, C, C, mine, other),
         [pl.BlockSpec((1, block, block), lambda i, s: (s[i], s[2 * m], 0)),
          pl.BlockSpec((1, block, block), lambda i, s: (s[i], 1 - s[2 * m], 0)),
-         pl.BlockSpec((block, block), lambda i, s: (s[2 * m], s[m + i])),
-         pl.BlockSpec((block, block), lambda i, s: (1 - s[2 * m], s[m + i])),
+         pl.BlockSpec((1, block, block), lambda i, s: (s[m + i], s[2 * m], 0)),
+         pl.BlockSpec((1, block, block), lambda i, s: (s[m + i], 1 - s[2 * m], 0)),
          full, full],
         jax.ShapeDtypeStruct((m * block, n3), BF), pl.BlockSpec((block, n3), lambda i, s: (i, 0)), (m,), (), 4 * m * block * block * n3)
 
@@ -223,68 +231,68 @@
     blocks = lambda flip: ints(*[q * 4 + ((p + yh + flip) % 2) * 2 + c for q in range(4) for p in range(2)])
     keepA, sendA = chunk(0, split, *weights)
 
-    *weights, cotangent = after((*weights, cotangent), sendA)
+    cotangent, = after((cotangent,), sendA)
     gotA = across(sendA)
-    eighth = rows // 8
-    part = columns(lax.dynamic_slice_in_dim(cotangent, (z * 2 + 1 - yl) * eighth, eighth, 0), blocks(1), width)
+    part = columns(cotangent, blocks(1), width, 1 - yl, half, half)
+    C = columns(cotangent, blocks(0), width, 0 * z, rows, pair)
+    ownA = cat(keepA, gotA)
+
+    ownA, tokens, C, part, *weights = after((ownA, tokens, C, part, *weights))
+    keepB, sendB = chunk(split, F, *weights)
+    WA = lax.all_gather(ownA, "x", axis=0, tiled=True)
+    near, off, opposite = beside(tokens), behind(tokens), across(tokens)
+    here = cat(ordered(first, tokens, near, 1), ordered(first, opposite, off, 1))
+
+    here, part, keepB, sendB = after((here, part, keepB, sendB))
+    z_before, z_after = ring(here, "z", 1), ring(here, "z", -1)
+    ownB = cat(keepB, across(sendB))
     part = behind(part)
-    C = columns(cotangent, blocks(0), width, pair)
-    keepB, sendB = chunk(split, F, *weights)
-    ownA = cat(keepA, gotA)
-
-    ownA, tokens, part, C, keepB, sendB = after((ownA, tokens, part, C, keepB, sendB))
-    WA = lax.all_gather(ownA, "x", axis=0, tiled=True)
-    near, off, opposite, part2 = beside(tokens), behind(tokens), across(tokens), beside(part)
-    here = cat(ordered(first, tokens, near, 1), ordered(first, opposite, off, 1))
-    part = ordered(yl == 0, part, part2, 0)
-
-    here, part = after((here, part))
-    z_before, z_after = ring(here, "z", 1), ring(here, "z", -1)
-    c_before, c_after = ring(part, "z", 1), ring(part, "z", -1)
-
-    z_before, z_after, c_before, c_after, sendB = after((z_before, z_after, c_before, c_after, sendB))
+
+    z_before, z_after = after((z_before, z_after))
     up, down = ring(z_before[:rows], "z", 1), ring(z_after[rows:], "z", -1)
-    c_up, c_down = ring(c_before[:eighth], "z", 1), ring(c_after[eighth:], "z", -1)
-    ownB = cat(keepB, across(sendB))
-    stack = cat(here, z_after, up, down, z_before)
-    X = stack.reshape(4, pair, block)
-    for j, v in enumerate((part, c_after, (c_up, c_down), c_before)):
-        for i, v in enumerate(v if j == 2 else (v,)):
-            C = lax.dynamic_update_slice_in_dim(C, v, rows + (z + j) % 4 * 2 * eighth + i * eighth, 0)
-
-    ownB, stack, C = after((ownB, stack, C), WA)
-    X = stack.reshape(4, pair, block)
+    rest = beside(part)
+    X = cat(here, z_after, up, down, z_before).reshape(4, pair, block)
+
+    ownB, part = after((ownB, part), up, down)
+    ownB, WA = after((ownB, WA))
     WB = lax.all_gather(ownB, "x", axis=0, tiled=True)
+    for i, v in ((yl, part), (1 - yl, rest)):
+        C = lax.dynamic_update_slice_in_dim(C, v, rows + i * half, 1)
 
     def compute(W):
         theirs, mine = partial_x(X, W, places)
         theirs_d, mine_d = partial_c(C, W, ints(c))
         mine = activate(mine, sibling(theirs), mine_d, sibling(theirs_d), ints(c))
-        other = sibling(mine)
-        return mine, other, grads(X, C, mine, other, x_of, c, (0, 1, 2, 3))
-
-    *A, termsA = compute(WA)
+        return mine, sibling(mine)
+
+    A = compute(WA)
+    termsA = grads(X, C, *A, x_of, c, (0, 1, 2, 3))
     sumA = lax.psum_scatter(termsA, "x", scatter_dimension=0, tiled=True)
     WB, X, C = after((WB, X, C), termsA)
-    *B, termsB = compute(WB)
+    B = compute(WB)
+
+    far = d_x(WA, WB, A, B, w_of, c, (2,))
+    X, C, *B = after((X, C, *B), far)
+    up, down = ring(far[:rows], "z", 1), ring(far[rows:], "z", -1)
+
+    termsB = grads(X, C, *B, x_of, c, (0, 1, 2, 3))
     sumB = lax.psum_scatter(termsB, "x", scatter_dimension=0, tiled=True)
-
-    A, B = after((*A, *B), termsB)[:2], after((*A, *B), termsB)[2:]
-    dx = d_x(WA, WB, A, B, w_of, c, (2, 1, 3, 0))
-    up, down = ring(dx[:rows], "z", 1), ring(dx[rows:pair], "z", -1)
-    terms = dx[pair:]
-    one, three = merge(terms, up, down)
+    B = after(B, termsB)
+    dx = d_x(WA, WB, A, B, w_of, c, (1, 3, 0))
+
+    one, three = merge(dx, up, down)
     up, down = ring(one, "z", 1), ring(three, "z", -1)
-    dx = terms[2 * pair:].astype(F32) + up.astype(F32) + down.astype(F32)
+    gotA = across(sumA[half:])
+    up, down, gotA = after((up, down, gotA))
+    dx = dx[2 * pair:].astype(F32) + up.astype(F32) + down.astype(F32)
     mine, theirs = jnp.where(first, dx[:, :width], dx[:, width:]), jnp.where(first, dx[:, width:], dx[:, :width]).astype(BF)
-    gotA = across(sumA[half:])
+
     near, off, opposite = beside(theirs[:rows]), behind(theirs[rows:]), across(mine[rows:].astype(BF))
+
+    sumA = give_back(*after((sumA[:half], gotA), near, off, opposite))
+    sumB, near, off, opposite = after((sumB, near, off, opposite), sumA)
+    sumB = give_back(sumB[:half], across(sumB[half:]))
     d_tokens = mine[:rows] + near.astype(F32) + off.astype(F32) + opposite.astype(F32)
-    sumA = give_back(sumA[:half], gotA)
-
-    sumB, = after((sumB,), d_tokens, sumA)
-    gotB = across(sumB[half:])
-    sumB = give_back(sumB[:half], gotB)
     n, m = split, F - split
     gate, up, down = (cat(sumA[:, i * n:(i + 1) * n], sumB[:, i * m:(i + 1) * m], axis=1) for i in range(3))
     return d_tokens.astype(BF), gate, up, down.T

time: 342 us -> 315 us (0.921)
  local copies, waits for them, and re-layouts: 40.5 us -> 30.5 us
  waiting for transfers between devices: 128 us -> 118 us
  starting transfers between devices: 47.9 us -> 40.9 us
  Pallas kernels: 91.6 us -> 96.8 us
  other arithmetic: 18.3 us -> 13.9 us
    ppermute x3, waiting for transfers between devices: 6.84 us -> 22.3 us  [behind(): return lax.ppermute(v, ('yl', 'yh'), [(0, 3), (3, 0), (1, 2), (2, 1)])]
    all_gather x1, waiting for transfers between devices: 12.3 us -> 0.02 us  [per_device(): WB = lax.all_gather(ownB, 'x', axis=0, tiled=True)]
    ppermute x12 -> x8, waiting for transfers between devices: 57.1 us -> 45.6 us  [ring(): return lax.ppermute(v, axis, [(i, (i + step) % 4) for i in range(4)])]
    slice x7 -> x4, local copies, waits for them, and re-layouts: 10.1 us -> 2.69 us  [the longest x1 1.47 us: per_device(): sumA = give_back(*after((sumA[:half], gotA), near, off, opposite))]
    ppermute x12 -> x8, starting transfers between devices: 17.6 us -> 10.9 us  [ring(): return lax.ppermute(v, axis, [(i, (i + step) % 4) for i in range(4)])]
    pallas_call x12 -> x13, Pallas kernels: 91.6 us -> 96.8 us  [call(): pl.pallas_call(body, grid_spec=pltpu.PrefetchScalarGridSpec(num_scalar_pr...]
    dynamic_update_slice x5 -> x2, local copies, waits for them, and re-layouts: 7.21 us -> 4.55 us  [per_device(): C = lax.dynamic_update_slice_in_dim(C, v, rows + i * half, 1)]
    unnamed x37 -> x49, local copies, waits for them, and re-layouts: 13.5 us -> 15.5 us
  transfers between devices with their start and end apart: 38 -> 34, of which waited for: 23 -> 22; matrix products, arithmetic and copies ran while one was open for 11% -> 7% of each run, Pallas kernels for 27% -> 31%
where the time goes in v2:
time: 315 us; the launch traced here: 314 us
  waiting for transfers between devices  118 us (37%)
  Pallas kernels  96.8 us (31%)
  starting transfers between devices  40.9 us (13%)
  local copies, waits for them, and re-layouts  30.5 us (10%)
  between operations  14.2 us (5%)
  other arithmetic  13.9 us (4%)
    pallas_call x13, Pallas kernels, call(): pl.pallas_call(body, grid_spec=pltpu.PrefetchScalarGridSpec(num_scalar_pr...  96.8 us
    ppermute x8, waiting for transfers between devices, ring(): return lax.ppermute(v, axis, [(i, (i + step) % 4) for i in range(4)])  45.6 us
    ppermute x6, waiting for transfers between devices, across(): return lax.ppermute(v, 'yh', SWAP)  27.3 us
    ppermute x3, waiting for transfers between devices, behind(): return lax.ppermute(v, ('yl', 'yh'), [(0, 3), (3, 0), (1, 2), (2, 1)])  22.3 us
    unnamed x49, local copies, waits for them, and re-layouts  15.5 us
    ppermute x6, starting transfers between devices, across(): return lax.ppermute(v, 'yh', SWAP)  14.3 us
    ppermute x10, waiting for transfers between devices, sibling(): return lax.ppermute(v, 'c', SWAP)  11.8 us
    ppermute x8, starting transfers between devices, ring(): return lax.ppermute(v, axis, [(i, (i + step) % 4) for i in range(4)])  10.9 us
  transfers between devices with their start and end apart: 34, of which 22 were waited for; matrix products, arithmetic and copies ran while one was open for 7% of the time, Pallas kernels for 31%

profile of v2, /device:TPU:1, one launch (start us, length us, event | category | flops | bytes accessed | tf_op | source)
XLA Modules:
  0.0 314.0 jit_solution(1061549790336473716)
XLA Ops:
  14.5 3.1 collective-permute-start.1
  18.8 5.9 %columns.3 = bf16[4,256,512]{2,1,0:T(8,128)(2,1)} custom-call(s32[9]{0:T(128)} %concatenate.67.places, bf16[512,4096]{1,0:T(8,128)(2,1)} %src.1), custom_call_target="tpu_custom_call" | custom-call | bytes 52428 | tf_op jit(solution)/shard_map/columns/pallas_call | solution.py:60
  24.7 6.4 %columns.2 = bf16[4,1024,512]{2,1,0:T(8,128)(2,1)} custom-call(s32[9]{0:T(128)} %concatenate.66.places, bf16[512,4096]{1,0:T(8,128)(2,1)} %src.1), custom_call_target="tpu_custom_call" | custom-call | bytes 83886 | tf_op jit(solution)/shard_map/columns/pallas_call | solution.py:60
  31.2 3.7 %collective-permute-done.1 = bf16[256,1536]{1,0:T(8,128)(2,1)S(1)} collective-permute-done((bf16[256,1536]{1,0:T(8,128)(2,1)S(1)}, bf16[256,1536]{1,0:T(8,128)(2,1)S(1)}, u32[]{:S(2)}, u32[]{:S(2)}) %collective-permute-start.1) | collective-permute-done | bytes 786464 | tf_op jit(solution)/shard_map/ppermute | solution.py:26
  43.8 7.3 %collective-permute-done.3 = bf16[512,256]{1,0:T(8,128)(2,1)S(1)} collective-permute-done((bf16[512,256]{1,0:T(8,128)(2,1)S(1)}, bf16[512,256]{1,0:T(8,128)(2,1)S(1)}, u32[]{:S(2)}, u32[]{:S(2)}) %collective-permute-start.3) | collective-permute-done | bytes 262176 | tf_op jit(solution)/shard_map/ppermute | solution.py:26
  51.1 6.1 %collective-permute-done.4 = bf16[512,256]{1,0:T(8,128)(2,1)S(1)} collective-permute-done((bf16[512,256]{1,0:T(8,128)(2,1)S(1)}, bf16[512,256]{1,0:T(8,128)(2,1)S(1)}, u32[]{:S(2)}, u32[]{:S(2)}) %collective-permute-start.4) | collective-permute-done | bytes 262176 | tf_op jit(solution)/shard_map/ppermute | solution.py:34
  57.7 3.8 %collective-permute-start.9 = (bf16[1024,512]{1,0:T(8,128)(2,1)S(1)}, bf16[1024,512]{1,0:T(8,128)(2,1)S(1)}, u32[]{:S(2)}, u32[]{:S(2)}) collective-permute-start(bf16[1024,512]{1,0:T(8,128)(2,1)S(1)} %pad_maximum_fusion.2), channel_id=1, source_target_pairs={{0,96},{32,0},{64,32},{96,64},{1,97},{33,1},{65,33},{97,65},{2,98}... | collective-permute-start | bytes 3145736 | tf_op jit(solution)/shard_map/ppermute | solution.py:18
  62.8 20.5 %collective-permute-done.9 = bf16[1024,512]{1,0:T(8,128)(2,1)S(1)} collective-permute-done((bf16[1024,512]{1,0:T(8,128)(2,1)S(1)}, bf16[1024,512]{1,0:T(8,128)(2,1)S(1)}, u32[]{:S(2)}, u32[]{:S(2)}) %collective-permute-start.9) | collective-permute-done | bytes 1048608 | tf_op jit(solution)/shard_map/ppermute | solution.py:18
  83.3 3.2 %collective-permute-done.8 = bf16[1024,512]{1,0:T(8,128)(2,1)S(1)} collective-permute-done((bf16[1024,512]{1,0:T(8,128)(2,1)S(1)}, bf16[1024,512]{1,0:T(8,128)(2,1)S(1)}, u32[]{:S(2)}, u32[]{:S(2)}) %collective-permute-start.8) | collective-permute-done | bytes 1048608 | tf_op jit(solution)/shard_map/ppermute | solution.py:18
  90.7 8.7 %collective-permute-done.7 = bf16[4,256,512]{2,1,0:T(8,128)(2,1)} collective-permute-done((bf16[4,256,512]{2,1,0:T(8,128)(2,1)}, bf16[4,256,512]{2,1,0:T(8,128)(2,1)}, u32[]{:S(2)}, u32[]{:S(2)}) %collective-permute-start.7) | collective-permute-done | bytes 1048608 | tf_op jit(solution)/shard_map/ppermute | solution.py:34
  101.7 3.3 %all-gather.3.cloned.1.call-done.w.wa = bf16[2048,1536]{1,0:T(8,128)(2,1)} async-done(((bf16[512,1536]{1,0:T(8,128)(2,1)}), bf16[2048,1536]{1,0:T(8,128)(2,1)}) %all-gather.3.cloned.1.call-update) | async-done | bytes 6291472 | tf_op jit(solution)/shard_map/all_gather | solution.py:242
  111.4 9.2 %partial_x.2 = (bf16[512,1024]{1,0:T(8,128)(2,1)}, f32[512,1024]{1,0:T(8,128)}) custom-call(s32[5]{0:T(128)} %stack.122.places, bf16[4,1024,512]{2,1,0:T(8,128)(2,1)} %bitcast.31, bf16[4,1024,512]{2,1,0:T(8,128)(2,1)} %bitcast.32, bf16[4,1024,512]{2,1,0:T(8,128)(2,1)} %bitcast.33, bf16[4,1024,512]{2,1,0:T(8,128)(2,1)} %bitcast.34, ...), custom_call_target="tpu_custom_call" | custom-call | flops 64424508 | bytes 262144 | tf_op jit(solution)/shard_map/partial_x/pallas_call | solution.py:60
  123.8 6.2 %collective-permute-done.12 = bf16[4,256,512]{2,1,0:T(8,128)(2,1)} collective-permute-done((bf16[4,256,512]{2,1,0:T(8,128)(2,1)}, bf16[4,256,512]{2,1,0:T(8,128)(2,1)}, u32[]{:S(2)}, u32[]{:S(2)}) %collective-permute-start.12) | collective-permute-done | bytes 1048608 | tf_op jit(solution)/shard_map/ppermute | solution.py:30
  132.3 6.0 %partial_c.2 = (bf16[512,512]{1,0:T(8,128)(2,1)}, f32[512,512]{1,0:T(8,128)}) custom-call(s32[1]{0:T(128)} %bitcast.3.places, bf16[4,1024,512]{2,1,0:T(8,128)(2,1)} %constant_dynamic-update-slice_fusion.5.cot.cm.co, bf16[2048,1536]{1,0:T(8,128)(2,1)} %all-gather.3.cloned.1.call-done.w.wa), custom_call_target="tpu_custom_call" | custom-call | flops 21474836 | bytes 120586 | tf_op jit(solution)/shard_map/partial_c/pallas_call | solution.py:60
  142.7 4.4 %activate.2.dm.ma = bf16[512,1536]{1,0:T(8,128)(2,1)} custom-call(s32[1]{0:T(128)} %bitcast.3.places, f32[512,1024]{1,0:T(8,128)} %get-tuple-element.68.mine, bf16[512,1024]{1,0:T(8,128)(2,1)} %copy-done.6, f32[512,512]{1,0:T(8,128)} %get-tuple-element.70.mine_d, bf16[512,512]{1,0:T(8,128)(2,1)} %copy-done.12), custom_call_target="tpu_custom_call" | custom-call | flops 78643 | bytes 62914 | tf_op jit(solution)/shard_map/activate/pallas_call | solution.py:60
  152.0 12.3 %grads.2 = bf16[2048,1536]{1,0:T(8,128)(2,1)} custom-call(s32[10]{0:T(128)} %stack.121.places, bf16[4,1024,512]{2,1,0:T(8,128)(2,1)} %bitcast.35, bf16[4,1024,512]{2,1,0:T(8,128)(2,1)} %bitcast.36, bf16[4,1024,512]{2,1,0:T(8,128)(2,1)} %constant_dynamic-update-slice_fusion.5.cot.cm.co, bf16[4,1024,512]{2,1,0:T(8,128)(2,1)} %constant_dynamic-update-slice_fusion.5.cot.cm.co, ...), custom_call_target="tpu_custom_call" | custom-call | flops 64424508 | bytes 262144 | tf_op jit(solution)/shard_map/grads/pallas_call | solution.py:60
  164.6 9.0 %partial_x.3 = (bf16[512,768]{1,0:T(8,128)(2,1)}, f32[512,768]{1,0:T(8,128)}) custom-call(s32[5]{0:T(128)} %stack.122.places, bf16[4,1024,512]{2,1,0:T(8,128)(2,1)} %bitcast.37, bf16[4,1024,512]{2,1,0:T(8,128)(2,1)} %bitcast.38, bf16[4,1024,512]{2,1,0:T(8,128)(2,1)} %bitcast.39, bf16[4,1024,512]{2,1,0:T(8,128)(2,1)} %bitcast.40, ...), custom_call_target="tpu_custom_call" | custom-call | flops 48318384 | bytes 238551 | tf_op jit(solution)/shard_map/partial_x/pallas_call | solution.py:60
  173.9 6.5 %partial_c.3 = (bf16[512,384]{1,0:T(8,128)(2,1)}, f32[512,384]{1,0:T(8,128)}) custom-call(s32[1]{0:T(128)} %bitcast.3.places, bf16[4,1024,512]{2,1,0:T(8,128)(2,1)} %constant_dynamic-update-slice_fusion.5.cot.cm.co, bf16[2048,1152]{1,0:T(8,128)(2,1)} %all-gather.5.cloned.1.call-done.w.wb), custom_call_target="tpu_custom_call" | custom-call | flops 16106127 | bytes 100925 | tf_op jit(solution)/shard_map/partial_c/pallas_call | solution.py:60
  183.3 4.1 %activate.3.mb.dm = bf16[512,1152]{1,0:T(8,128)(2,1)} custom-call(s32[1]{0:T(128)} %bitcast.3.places, f32[512,768]{1,0:T(8,128)} %get-tuple-element.75.mine, bf16[512,768]{1,0:T(8,128)(2,1)} %copy-done.7, f32[512,384]{1,0:T(8,128)} %get-tuple-element.77.mine_d, bf16[512,384]{1,0:T(8,128)(2,1)} %copy-done.13), custom_call_target="tpu_custom_call" | custom-call | flops 58982 | bytes 47185 | tf_op jit(solution)/shard_map/activate/pallas_call | solution.py:60
  191.5 7.1 %d_x.2 = bf16[1024,512]{1,0:T(8,128)(2,1)} custom-call(s32[2]{0:T(128)} %pad_add_fusion.1.places, bf16[2048,1536]{1,0:T(8,128)(2,1)} %all-gather.3.cloned.1.call-done.w.wa, bf16[2048,1152]{1,0:T(8,128)(2,1)} %all-gather.5.cloned.1.call-done.w.wb, bf16[512,1536]{1,0:T(8,128)(2,1)} %activate.2.dm.ma, bf16[512,1536]{1,0:T(8,128)(2,1)} %copy-done.1, ...), custom_call_target="tpu_custom_call" | custom-call | flops 18790480 | bytes 175636 | tf_op jit(solution)/shard_map/d_x/pallas_call | solution.py:60
  198.6 11.0 %grads.3 = bf16[2048,1152]{1,0:T(8,128)(2,1)} custom-call(s32[10]{0:T(128)} %stack.121.places, bf16[4,1024,512]{2,1,0:T(8,128)(2,1)} %bitcast.41, bf16[4,1024,512]{2,1,0:T(8,128)(2,1)} %bitcast.42, bf16[4,1024,512]{2,1,0:T(8,128)(2,1)} %constant_dynamic-update-slice_fusion.5.cot.cm.co, bf16[4,1024,512]{2,1,0:T(8,128)(2,1)} %constant_dynamic-update-slice_fusion.5.cot.cm.co, ...), custom_call_target="tpu_custom_call" | custom-call | flops 48318384 | bytes 238551 | tf_op jit(solution)/shard_map/grads/pallas_call | solution.py:60
  210.9 2.9 collective-permute-start.20
  214.4 11.6 %d_x.3.terms = bf16[3072,512]{1,0:T(8,128)(2,1)} custom-call(s32[4]{0:T(128)} %pad_add_fusion.places, bf16[2048,1536]{1,0:T(8,128)(2,1)} %all-gather.3.cloned.1.call-done.w.wa, bf16[2048,1152]{1,0:T(8,128)(2,1)} %all-gather.5.cloned.1.call-done.w.wb, bf16[512,1536]{1,0:T(8,128)(2,1)} %activate.2.dm.ma, bf16[512,1536]{1,0:T(8,128)(2,1)} %copy-done.1, ...), custom_call_target="tpu_custom_call" | custom-call | flops 56371444 | bytes 196608 | tf_op jit(solution)/shard_map/d_x/pallas_call | solution.py:60
  228.7 3.3 %merge.1 = (bf16[1024,512]{1,0:T(8,128)(2,1)}, bf16[1024,512]{1,0:T(8,128)(2,1)}) custom-call(s32[1]{0:T(128)} %constant.121.clone.1.places, bf16[3072,512]{1,0:T(8,128)(2,1)} %d_x.3.terms, bf16[512,512]{1,0:T(8,128)(2,1)} %copy-done.11, bf16[512,512]{1,0:T(8,128)(2,1)} %copy-done.10), custom_call_target="tpu_custom_call" | custom-call | bytes 62914 | tf_op jit(solution)/shard_map/merge/pallas_call | solution.py:60
  232.0 2.7 collective-permute-start.22
  236.2 2.8 collective-permute-start.23
  239.0 17.8 %collective-permute-done.21 = bf16[1024,512]{1,0:T(8,128)(2,1)S(1)} collective-permute-done((bf16[1024,512]{1,0:T(8,128)(2,1)}, bf16[1024,512]{1,0:T(8,128)(2,1)S(1)}, u32[]{:S(2)}, u32[]{:S(2)}) %collective-permute-start.21) | collective-permute-done | bytes 1048608 | tf_op jit(solution)/shard_map/ppermute | solution.py:18
  258.6 2.8 collective-permute-start.26
  262.5 3.2 %collective-permute-done.26 = bf16[512,256]{1,0:T(8,128)(2,1)S(1)} collective-permute-done((bf16[512,256]{1,0:T(8,128)(2,1)S(1)}, bf16[512,256]{1,0:T(8,128)(2,1)S(1)}, u32[]{:S(2)}, u32[]{:S(2)}) %collective-permute-start.26) | collective-permute-done | bytes 262176 | tf_op jit(solution)/shard_map/ppermute | solution.py:26
  265.7 7.5 %collective-permute-done.25 = bf16[512,256]{1,0:T(8,128)(2,1)S(1)} collective-permute-done((bf16[512,256]{1,0:T(8,128)(2,1)S(1)}, bf16[512,256]{1,0:T(8,128)(2,1)S(1)}, u32[]{:S(2)}, u32[]{:S(2)}) %collective-permute-start.25) | collective-permute-done | bytes 262176 | tf_op jit(solution)/shard_map/ppermute | solution.py:34
  283.1 2.8 collective-permute-start.28
  285.9 13.0 %collective-permute-done.28 = bf16[256,1152]{1,0:T(8,128)(2,1)S(1)} collective-permute-done((bf16[256,1152]{1,0:T(8,128)(2,1)S(1)}, bf16[256,1152]{1,0:T(8,128)(2,1)S(1)}, u32[]{:S(2)}, u32[]{:S(2)}) %collective-permute-start.28) | collective-permute-done | bytes 589856 | tf_op jit(solution)/shard_map/ppermute | solution.py:26
  (157 shorter events, 81.5 us)
Async XLA Ops:
  7.2 97.8 %all-gather.3.cloned.1.call-start = ((), (), s32[]{:S(2)}) async-start(), calls=%async_computation.2 | async-start | bytes 7864320 | tf_op jit(solution)/shard_map/all_gather | solution.py:242
  8.8 3.4 %collective-permute-start = (bf16[256,1536]{1,0:T(8,128)(2,1)S(1)}, bf16[256,1536]{1,0:T(8,128)(2,1)S(1)}, u32[]{:S(2)}, u32[]{:S(2)}) collective-permute-start(bf16[256,1536]{1,0:T(8,128)(2,1)S(1)} %pad_maximum_fusion.6), channel_id=1, source_target_pairs={{0,8},{8,0},{1,9},{9,1},{2,10},{10,2},{3,11},{11,3},{4,12},{12,4},... | collective-permute-start | bytes 2359304 | tf_op jit(solution)/shard_map/ppermute | solution.py:22
  14.5 20.4 %collective-permute-start.1 = (bf16[256,1536]{1,0:T(8,128)(2,1)S(1)}, bf16[256,1536]{1,0:T(8,128)(2,1)S(1)}, u32[]{:S(2)}, u32[]{:S(2)}) collective-permute-start(bf16[256,1536]{1,0:T(8,128)(2,1)S(1)} %get-tuple-element.110), channel_id=1, source_target_pairs={{0,1},{1,0},{2,3},{3,2},{4,5},{5,4},{6,7},{7,6},{8,9},{9,8},{10,11... | collective-permute-start | bytes 2359304 | tf_op jit(solution)/shard_map/ppermute | solution.py:26
  36.3 128.3 %all-gather.5.cloned.1.call-start = ((), (), s32[]{:S(2)}) async-start(), calls=%async_computation.3 | async-start | bytes 5898240 | tf_op jit(solution)/shard_map/all_gather | solution.py:258
  36.3 7.4 %collective-permute-start.2 = (bf16[512,256]{1,0:T(8,128)(2,1)S(1)}, bf16[512,256]{1,0:T(8,128)(2,1)S(1)}, u32[]{:S(2)}, u32[]{:S(2)}) collective-permute-start(bf16[512,256]{1,0:T(8,128)(2,1)S(1)} %copy-done.14), channel_id=1, source_target_pairs={{0,16},{16,0},{1,17},{17,1},{2,18},{18,2},{3,19},{19,3},{4,20},{20... | collective-permute-start | bytes 786440 | tf_op jit(solution)/shard_map/ppermute | solution.py:30
  39.0 18.5 %collective-permute-start.5 = (bf16[256,1152]{1,0:T(8,128)(2,1)S(1)}, bf16[256,1152]{1,0:T(8,128)(2,1)S(1)}, u32[]{:S(2)}, u32[]{:S(2)}) collective-permute-start(bf16[256,1152]{1,0:T(8,128)(2,1)S(1)} %pad_maximum_fusion.8), channel_id=1, source_target_pairs={{0,8},{8,0},{1,9},{9,1},{2,10},{10,2},{3,11},{11,3},{4,12},{12,4},... | collective-permute-start | bytes 1769480 | tf_op jit(solution)/shard_map/ppermute | solution.py:22
  40.5 10.6 %collective-permute-start.3 = (bf16[512,256]{1,0:T(8,128)(2,1)S(1)}, bf16[512,256]{1,0:T(8,128)(2,1)S(1)}, u32[]{:S(2)}, u32[]{:S(2)}) collective-permute-start(bf16[512,256]{1,0:T(8,128)(2,1)S(1)} %copy-done.14), channel_id=1, source_target_pairs={{0,1},{1,0},{2,3},{3,2},{4,5},{5,4},{6,7},{7,6},{8,9},{9,8},{10,11... | collective-permute-start | bytes 786440 | tf_op jit(solution)/shard_map/ppermute | solution.py:26
  43.2 14.1 %collective-permute-start.4 = (bf16[512,256]{1,0:T(8,128)(2,1)S(1)}, bf16[512,256]{1,0:T(8,128)(2,1)S(1)}, u32[]{:S(2)}, u32[]{:S(2)}) collective-permute-start(bf16[512,256]{1,0:T(8,128)(2,1)S(1)} %copy-done.14), channel_id=1, source_target_pairs={{0,17},{17,0},{1,16},{16,1},{2,19},{19,2},{3,18},{18,3},{4,21},{21... | collective-permute-start | bytes 786440 | tf_op jit(solution)/shard_map/ppermute | solution.py:34
  57.7 25.7 %collective-permute-start.9 = (bf16[1024,512]{1,0:T(8,128)(2,1)S(1)}, bf16[1024,512]{1,0:T(8,128)(2,1)S(1)}, u32[]{:S(2)}, u32[]{:S(2)}) collective-permute-start(bf16[1024,512]{1,0:T(8,128)(2,1)S(1)} %pad_maximum_fusion.2), channel_id=1, source_target_pairs={{0,96},{32,0},{64,32},{96,64},{1,97},{33,1},{65,33},{97,65},{2,98}... | collective-permute-start | bytes 3145736 | tf_op jit(solution)/shard_map/ppermute | solution.py:18
  61.5 25.0 %collective-permute-start.8 = (bf16[1024,512]{1,0:T(8,128)(2,1)S(1)}, bf16[1024,512]{1,0:T(8,128)(2,1)S(1)}, u32[]{:S(2)}, u32[]{:S(2)}) collective-permute-start(bf16[1024,512]{1,0:T(8,128)(2,1)S(1)} %pad_maximum_fusion.2), channel_id=1, source_target_pairs={{0,32},{32,64},{64,96},{96,0},{1,33},{33,65},{65,97},{97,1},{2,34}... | collective-permute-start | bytes 3145736 | tf_op jit(solution)/shard_map/ppermute | solution.py:18
  61.5 37.9 %collective-permute-start.7 = (bf16[4,256,512]{2,1,0:T(8,128)(2,1)}, bf16[4,256,512]{2,1,0:T(8,128)(2,1)}, u32[]{:S(2)}, u32[]{:S(2)}) collective-permute-start(bf16[4,256,512]{2,1,0:T(8,128)(2,1)} %columns.3), channel_id=1, source_target_pairs={{0,17},{17,0},{1,16},{16,1},{2,19},{19,2},{3,18},{18,3},{4,21},{21... | collective-permute-start | bytes 3145736 | tf_op jit(solution)/shard_map/ppermute | solution.py:34
  62.6 27.0 %collective-permute-start.6 = (bf16[256,1152]{1,0:T(8,128)(2,1)S(1)}, bf16[256,1152]{1,0:T(8,128)(2,1)S(1)}, u32[]{:S(2)}, u32[]{:S(2)}) collective-permute-start(bf16[256,1152]{1,0:T(8,128)(2,1)S(1)} %get-tuple-element.57), channel_id=1, source_target_pairs={{0,1},{1,0},{2,3},{3,2},{4,5},{5,4},{6,7},{7,6},{8,9},{9,8},{10,11... | collective-permute-start | bytes 1769480 | tf_op jit(solution)/shard_map/ppermute | solution.py:26
  88.2 12.0 %collective-permute-start.11 = (bf16[512,512]{1,0:T(8,128)(2,1)}, bf16[512,512]{1,0:T(8,128)(2,1)}, u32[]{:S(2)}, u32[]{:S(2)}) collective-permute-start(bf16[512,512]{1,0:T(8,128)(2,1)} %slice.97), channel_id=1, source_target_pairs={{0,96},{32,0},{64,32},{96,64},{1,97},{33,1},{65,33},{97,65},{2,98}... | collective-permute-start | bytes 1572872 | tf_op jit(solution)/shard_map/ppermute | solution.py:18
  88.5 13.2 %collective-permute-start.10 = (bf16[512,512]{1,0:T(8,128)(2,1)}, bf16[512,512]{1,0:T(8,128)(2,1)}, u32[]{:S(2)}, u32[]{:S(2)}) collective-permute-start(bf16[512,512]{1,0:T(8,128)(2,1)} %slice.96), channel_id=1, source_target_pairs={{0,32},{32,64},{64,96},{96,0},{1,33},{33,65},{65,97},{97,1},{2,34}... | collective-permute-start | bytes 1572872 | tf_op jit(solution)/shard_map/ppermute | solution.py:18
  105.0 129.7 %reduce-scatter.3.cloned.1.call-start = ((), (), s32[]{:S(2)}) async-start(), calls=%async_computation.4 | async-start | bytes 7864320 | tf_op jit(solution)/shard_map/reduce_scatter | solution.py:270
  105.7 24.3 %collective-permute-start.12 = (bf16[4,256,512]{2,1,0:T(8,128)(2,1)}, bf16[4,256,512]{2,1,0:T(8,128)(2,1)}, u32[]{:S(2)}, u32[]{:S(2)}) collective-permute-start(bf16[4,256,512]{2,1,0:T(8,128)(2,1)} %collective-permute-done.7), channel_id=1, source_target_pairs={{0,16},{16,0},{1,17},{17,1},{2,18},{18,2},{3,19},{19,3},{4,20},{20... | collective-permute-start | bytes 3145736 | tf_op jit(solution)/shard_map/ppermute | solution.py:30
  120.6 21.0 %collective-permute-start.13 = (bf16[512,1024]{1,0:T(8,128)(2,1)}, bf16[512,1024]{1,0:T(8,128)(2,1)S(1)}, u32[]{:S(2)}, u32[]{:S(2)}) collective-permute-start(bf16[512,1024]{1,0:T(8,128)(2,1)} %get-tuple-element.69), channel_id=1, source_target_pairs={{0,8},{8,0},{1,9},{9,1},{2,10},{10,2},{3,11},{11,3},{4,12},{12,4},... | collective-permute-start | bytes 3145736 | tf_op jit(solution)/shard_map/ppermute | solution.py:22
  138.3 3.3 %collective-permute-start.14 = (bf16[512,512]{1,0:T(8,128)(2,1)}, bf16[512,512]{1,0:T(8,128)(2,1)S(1)}, u32[]{:S(2)}, u32[]{:S(2)}) collective-permute-start(bf16[512,512]{1,0:T(8,128)(2,1)} %get-tuple-element.71), channel_id=1, source_target_pairs={{0,8},{8,0},{1,9},{9,1},{2,10},{10,2},{3,11},{11,3},{4,12},{12,4},... | collective-permute-start | bytes 1572872 | tf_op jit(solution)/shard_map/ppermute | solution.py:22
  147.2 3.6 %collective-permute-start.15 = (bf16[512,1536]{1,0:T(8,128)(2,1)}, bf16[512,1536]{1,0:T(8,128)(2,1)S(1)}, u32[]{:S(2)}, u32[]{:S(2)}) collective-permute-start(bf16[512,1536]{1,0:T(8,128)(2,1)} %activate.2.dm.ma), channel_id=1, source_target_pairs={{0,8},{8,0},{1,9},{9,1},{2,10},{10,2},{3,11},{11,3},{4,12},{12,4},... | collective-permute-start | bytes 4718600 | tf_op jit(solution)/shard_map/ppermute | solution.py:22
  164.3 117.7 %reduce-scatter.5.cloned.1.call-start = ((), (), s32[]{:S(2)}) async-start(), calls=%async_computation.5 | async-start | bytes 5898240 | tf_op jit(solution)/shard_map/reduce_scatter | solution.py:279
  173.5 8.8 %collective-permute-start.16 = (bf16[512,768]{1,0:T(8,128)(2,1)}, bf16[512,768]{1,0:T(8,128)(2,1)S(1)}, u32[]{:S(2)}, u32[]{:S(2)}) collective-permute-start(bf16[512,768]{1,0:T(8,128)(2,1)} %get-tuple-element.76), channel_id=1, source_target_pairs={{0,8},{8,0},{1,9},{9,1},{2,10},{10,2},{3,11},{11,3},{4,12},{12,4},... | collective-permute-start | bytes 2359304 | tf_op jit(solution)/shard_map/ppermute | solution.py:22
  210.9 15.2 %collective-permute-start.20 = (bf16[512,512]{1,0:T(8,128)(2,1)S(1)}, bf16[512,512]{1,0:T(8,128)(2,1)S(1)}, u32[]{:S(2)}, u32[]{:S(2)}) collective-permute-start(bf16[512,512]{1,0:T(8,128)(2,1)S(1)} %get-tuple-element.116), channel_id=1, source_target_pairs={{0,96},{32,0},{64,32},{96,64},{1,97},{33,1},{65,33},{97,65},{2,98}... | collective-permute-start | bytes 1572872 | tf_op jit(solution)/shard_map/ppermute | solution.py:18
  213.8 14.1 %collective-permute-start.19 = (bf16[512,512]{1,0:T(8,128)(2,1)S(1)}, bf16[512,512]{1,0:T(8,128)(2,1)S(1)}, u32[]{:S(2)}, u32[]{:S(2)}) collective-permute-start(bf16[512,512]{1,0:T(8,128)(2,1)S(1)} %get-tuple-element.117), channel_id=1, source_target_pairs={{0,32},{32,64},{64,96},{96,0},{1,33},{33,65},{65,97},{97,1},{2,34}... | collective-permute-start | bytes 1572872 | tf_op jit(solution)/shard_map/ppermute | solution.py:18
  232.0 24.7 %collective-permute-start.21 = (bf16[1024,512]{1,0:T(8,128)(2,1)}, bf16[1024,512]{1,0:T(8,128)(2,1)S(1)}, u32[]{:S(2)}, u32[]{:S(2)}) collective-permute-start(bf16[1024,512]{1,0:T(8,128)(2,1)} %get-tuple-element.85), channel_id=1, source_target_pairs={{0,32},{32,64},{64,96},{96,0},{1,33},{33,65},{65,97},{97,1},{2,34}... | collective-permute-start | bytes 3145736 | tf_op jit(solution)/shard_map/ppermute | solution.py:18
  232.0 24.7 %collective-permute-start.22 = (bf16[1024,512]{1,0:T(8,128)(2,1)}, bf16[1024,512]{1,0:T(8,128)(2,1)S(1)}, u32[]{:S(2)}, u32[]{:S(2)}) collective-permute-start(bf16[1024,512]{1,0:T(8,128)(2,1)} %get-tuple-element.86), channel_id=1, source_target_pairs={{0,96},{32,0},{64,32},{96,64},{1,97},{33,1},{65,33},{97,65},{2,98}... | collective-permute-start | bytes 3145736 | tf_op jit(solution)/shard_map/ppermute | solution.py:18
  236.2 20.6 %collective-permute-start.23 = (bf16[256,1536]{1,0:T(8,128)(2,1)S(1)}, bf16[256,1536]{1,0:T(8,128)(2,1)S(1)}, u32[]{:S(2)}, u32[]{:S(2)}) collective-permute-start(bf16[256,1536]{1,0:T(8,128)(2,1)S(1)} %get-tuple-element.108), channel_id=1, source_target_pairs={{0,1},{1,0},{2,3},{3,2},{4,5},{5,4},{6,7},{7,6},{8,9},{9,8},{10,11... | collective-permute-start | bytes 2359304 | tf_op jit(solution)/shard_map/ppermute | solution.py:26
  258.6 7.1 %collective-permute-start.26 = (bf16[512,256]{1,0:T(8,128)(2,1)S(1)}, bf16[512,256]{1,0:T(8,128)(2,1)S(1)}, u32[]{:S(2)}, u32[]{:S(2)}) collective-permute-start(bf16[512,256]{1,0:T(8,128)(2,1)S(1)} %slice.150), channel_id=1, source_target_pairs={{0,1},{1,0},{2,3},{3,2},{4,5},{5,4},{6,7},{7,6},{8,9},{9,8},{10,11... | collective-permute-start | bytes 786440 | tf_op jit(solution)/shard_map/ppermute | solution.py:26
  261.6 11.7 %collective-permute-start.25 = (bf16[512,256]{1,0:T(8,128)(2,1)S(1)}, bf16[512,256]{1,0:T(8,128)(2,1)S(1)}, u32[]{:S(2)}, u32[]{:S(2)}) collective-permute-start(bf16[512,256]{1,0:T(8,128)(2,1)S(1)} %get-tuple-element.118), channel_id=1, source_target_pairs={{0,17},{17,0},{1,16},{16,1},{2,19},{19,2},{3,18},{18,3},{4,21},{21... | collective-permute-start | bytes 786440 | tf_op jit(solution)/shard_map/ppermute | solution.py:34
  262.5 10.8 %collective-permute-start.24 = (bf16[512,256]{1,0:T(8,128)(2,1)S(1)}, bf16[512,256]{1,0:T(8,128)(2,1)S(1)}, u32[]{:S(2)}, u32[]{:S(2)}) collective-permute-start(bf16[512,256]{1,0:T(8,128)(2,1)S(1)} %get-tuple-element.119), channel_id=1, source_target_pairs={{0,16},{16,0},{1,17},{17,1},{2,18},{18,2},{3,19},{19,3},{4,20},{20... | collective-permute-start | bytes 786440 | tf_op jit(solution)/shard_map/ppermute | solution.py:30
  274.8 3.5 %collective-permute-start.27 = (bf16[256,1536]{1,0:T(8,128)(2,1)S(1)}, bf16[256,1536]{1,0:T(8,128)(2,1)S(1)}, u32[]{:S(2)}, u32[]{:S(2)}) collective-permute-start(bf16[256,1536]{1,0:T(8,128)(2,1)S(1)} %get-tuple-element.106), channel_id=1, source_target_pairs={{0,8},{8,0},{1,9},{9,1},{2,10},{10,2},{3,11},{11,3},{4,12},{12,4},... | collective-permute-start | bytes 2359304 | tf_op jit(solution)/shard_map/ppermute | solution.py:22
  283.1 15.8 %collective-permute-start.28 = (bf16[256,1152]{1,0:T(8,128)(2,1)S(1)}, bf16[256,1152]{1,0:T(8,128)(2,1)S(1)}, u32[]{:S(2)}, u32[]{:S(2)}) collective-permute-start(bf16[256,1152]{1,0:T(8,128)(2,1)S(1)} %slice.111), channel_id=1, source_target_pairs={{0,1},{1,0},{2,3},{3,2},{4,5},{5,4},{6,7},{7,6},{8,9},{9,8},{10,11... | collective-permute-start | bytes 1769480 | tf_op jit(solution)/shard_map/ppermute | solution.py:26
  300.1 3.4 %collective-permute-start.29 = (bf16[256,1152]{1,0:T(8,128)(2,1)S(1)}, bf16[256,1152]{1,0:T(8,128)(2,1)S(1)}, u32[]{:S(2)}, u32[]{:S(2)}) collective-permute-start(bf16[256,1152]{1,0:T(8,128)(2,1)S(1)} %get-tuple-element.101), channel_id=1, source_target_pairs={{0,8},{8,0},{1,9},{9,1},{2,10},{10,2},{3,11},{11,3},{4,12},{12,4},... | collective-permute-start | bytes 1769480 | tf_op jit(solution)/shard_map/ppermute | solution.py:22
  (28 other events, 45.2 us)
Sparse Core Ops, SparseCore 0:
  36.4 68.5 all-gather.2
  106.6 53.2 all-gather.4
  164.4 64.3 reduce-scatter.2
  231.1 50.7 reduce-scatter.4

commit v3 on v2

--- a/solution.py
+++ b/solution.py
@@ -10,7 +10,7 @@
 BF = jnp.bfloat16
 F32 = jnp.float32
 SWAP = [(0, 1), (1, 0)]
-SPLIT = 512
+SPLIT = 384
 VMEM = 56 * 2**20
 
 
@@ -246,6 +246,7 @@
     here, part, keepB, sendB = after((here, part, keepB, sendB))
     z_before, z_after = ring(here, "z", 1), ring(here, "z", -1)
     ownB = cat(keepB, across(sendB))
+    ownB, part = after((ownB, part))
     part = behind(part)
 
     z_before, z_after = after((z_before, z_after))
@@ -253,8 +254,6 @@
     rest = beside(part)
     X = cat(here, z_after, up, down, z_before).reshape(4, pair, block)
 
-    ownB, part = after((ownB, part), up, down)
-    ownB, WA = after((ownB, WA))
     WB = lax.all_gather(ownB, "x", axis=0, tiled=True)
     for i, v in ((yl, part), (1 - yl, rest)):
         C = lax.dynamic_update_slice_in_dim(C, v, rows + i * half, 1)
@@ -294,8 +293,9 @@
     sumB = give_back(sumB[:half], across(sumB[half:]))
     d_tokens = mine[:rows] + near.astype(F32) + off.astype(F32) + opposite.astype(F32)
     n, m = split, F - split
-    gate, up, down = (cat(sumA[:, i * n:(i + 1) * n], sumB[:, i * m:(i + 1) * m], axis=1) for i in range(3))
-    return d_tokens.astype(BF), gate, up, down.T
+    gate, up = (cat(sumA[:, i * n:(i + 1) * n], sumB[:, i * m:(i + 1) * m], axis=1) for i in range(2))
+    down = cat(sumA[:, 2 * n:].T, sumB[:, 2 * m:].T)
+    return d_tokens.astype(BF), gate, up, down
 
 
 def solution(mesh):

time: 315 us -> 313 us (level)
  waiting for transfers between devices: 118 us -> 122 us
  other arithmetic: 13.9 us -> 10.6 us
  starting transfers between devices: 40.9 us -> 37.6 us
    ppermute x6, waiting for transfers between devices: 27.3 us -> 46.7 us  [across(): return lax.ppermute(v, 'yh', SWAP)]
    ppermute x3, waiting for transfers between devices: 22.3 us -> 9.72 us  [behind(): return lax.ppermute(v, ('yl', 'yh'), [(0, 3), (3, 0), (1, 2), (2, 1)])]
    all_gather x1, waiting for transfers between devices: 3.25 us -> 0.01 us  [per_device(): WA = lax.all_gather(ownA, 'x', axis=0, tiled=True)]
    unnamed x49 -> x43, local copies, waits for them, and re-layouts: 15.5 us -> 15.7 us
  transfers between devices with their start and end apart: 34 -> 34, of which waited for: 22 -> 20; matrix products, arithmetic and copies ran while one was open for 7% -> 8% of each run, Pallas kernels for 31% -> 31%
where the time goes in v3:
time: 313 us; the launch traced here: 312 us
  waiting for transfers between devices  122 us (39%)
  Pallas kernels  96.5 us (31%)
  starting transfers between devices  37.6 us (12%)
  local copies, waits for them, and re-layouts  31 us (10%)
  between operations  14.1 us (5%)
  other arithmetic  10.6 us (3%)
    pallas_call x13, Pallas kernels, call(): pl.pallas_call(body, grid_spec=pltpu.PrefetchScalarGridSpec(num_scalar_pr...  96.5 us
    ppermute x8, waiting for transfers between devices, ring(): return lax.ppermute(v, axis, [(i, (i + step) % 4) for i in range(4)])  48.5 us
    ppermute x6, waiting for transfers between devices, across(): return lax.ppermute(v, 'yh', SWAP)  46.7 us
    unnamed x43, local copies, waits for them, and re-layouts  15.7 us
    ppermute x10, waiting for transfers between devices, sibling(): return lax.ppermute(v, 'c', SWAP)  12.7 us
    ppermute x6, starting transfers between devices, across(): return lax.ppermute(v, 'yh', SWAP)  11.6 us
    ppermute x10, starting transfers between devices, sibling(): return lax.ppermute(v, 'c', SWAP)  11 us
    ppermute x8, starting transfers between devices, ring(): return lax.ppermute(v, axis, [(i, (i + step) % 4) for i in range(4)])  10.8 us
  transfers between devices with their start and end apart: 34, of which 20 were waited for; matrix products, arithmetic and copies ran while one was open for 8% of the time, Pallas kernels for 31%

profile of v3, /device:TPU:1, one launch (start us, length us, event | category | flops | bytes accessed | tf_op | source)
XLA Modules:
  0.0 311.5 jit_solution(3496786142540693449)
XLA Ops:
  12.0 3.1 collective-permute-start.1
  16.4 5.9 %columns.3 = bf16[4,256,512]{2,1,0:T(8,128)(2,1)} custom-call(s32[9]{0:T(128)} %concatenate.67.places, bf16[512,4096]{1,0:T(8,128)(2,1)} %src.1), custom_call_target="tpu_custom_call" | custom-call | bytes 52428 | tf_op jit(solution)/shard_map/columns/pallas_call | solution.py:60
  22.4 6.4 %columns.2 = bf16[4,1024,512]{2,1,0:T(8,128)(2,1)} custom-call(s32[9]{0:T(128)} %concatenate.66.places, bf16[512,4096]{1,0:T(8,128)(2,1)} %src.1), custom_call_target="tpu_custom_call" | custom-call | bytes 83886 | tf_op jit(solution)/shard_map/columns/pallas_call | solution.py:60
  34.4 2.6 collective-permute-start.3
  37.0 3.3 %collective-permute-done.2 = bf16[512,256]{1,0:T(8,128)(2,1)S(1)} collective-permute-done((bf16[512,256]{1,0:T(8,128)(2,1)S(1)}, bf16[512,256]{1,0:T(8,128)(2,1)S(1)}, u32[]{:S(2)}, u32[]{:S(2)}) %collective-permute-start.2) | collective-permute-done | bytes 262176 | tf_op jit(solution)/shard_map/ppermute | solution.py:30
  40.5 7.8 %collective-permute-done.3 = bf16[512,256]{1,0:T(8,128)(2,1)S(1)} collective-permute-done((bf16[512,256]{1,0:T(8,128)(2,1)S(1)}, bf16[512,256]{1,0:T(8,128)(2,1)S(1)}, u32[]{:S(2)}, u32[]{:S(2)}) %collective-permute-start.3) | collective-permute-done | bytes 262176 | tf_op jit(solution)/shard_map/ppermute | solution.py:26
  51.1 18.4 %collective-permute-done.6 = bf16[256,1536]{1,0:T(8,128)(2,1)S(1)} collective-permute-done((bf16[256,1536]{1,0:T(8,128)(2,1)S(1)}, bf16[256,1536]{1,0:T(8,128)(2,1)S(1)}, u32[]{:S(2)}, u32[]{:S(2)}) %collective-permute-start.6) | collective-permute-done | bytes 786464 | tf_op jit(solution)/shard_map/ppermute | solution.py:26
  70.9 3.8 %collective-permute-start.8 = (bf16[1024,512]{1,0:T(8,128)(2,1)S(1)}, bf16[1024,512]{1,0:T(8,128)(2,1)S(1)}, u32[]{:S(2)}, u32[]{:S(2)}) collective-permute-start(bf16[1024,512]{1,0:T(8,128)(2,1)S(1)} %pad_maximum_fusion.2), channel_id=1, source_target_pairs={{0,96},{32,0},{64,32},{96,64},{1,97},{33,1},{65,33},{97,65},{2,98}... | collective-permute-start | bytes 3145736 | tf_op jit(solution)/shard_map/ppermute | solution.py:18
  74.8 19.3 %collective-permute-done.8 = bf16[1024,512]{1,0:T(8,128)(2,1)S(1)} collective-permute-done((bf16[1024,512]{1,0:T(8,128)(2,1)S(1)}, bf16[1024,512]{1,0:T(8,128)(2,1)S(1)}, u32[]{:S(2)}, u32[]{:S(2)}) %collective-permute-start.8) | collective-permute-done | bytes 1048608 | tf_op jit(solution)/shard_map/ppermute | solution.py:18
  94.2 3.2 %collective-permute-done.7 = bf16[1024,512]{1,0:T(8,128)(2,1)S(1)} collective-permute-done((bf16[1024,512]{1,0:T(8,128)(2,1)S(1)}, bf16[1024,512]{1,0:T(8,128)(2,1)S(1)}, u32[]{:S(2)}, u32[]{:S(2)}) %collective-permute-start.7) | collective-permute-done | bytes 1048608 | tf_op jit(solution)/shard_map/ppermute | solution.py:18
  99.1 2.7 collective-permute-start.10
  104.5 4.6 %collective-permute-done.9 = bf16[512,512]{1,0:T(8,128)(2,1)} collective-permute-done((bf16[512,512]{1,0:T(8,128)(2,1)}, bf16[512,512]{1,0:T(8,128)(2,1)}, u32[]{:S(2)}, u32[]{:S(2)}) %collective-permute-start.9) | collective-permute-done | bytes 524320 | tf_op jit(solution)/shard_map/ppermute | solution.py:18
  113.9 9.1 %partial_x.2 = (bf16[512,768]{1,0:T(8,128)(2,1)}, f32[512,768]{1,0:T(8,128)}) custom-call(s32[5]{0:T(128)} %stack.122.places, bf16[4,1024,512]{2,1,0:T(8,128)(2,1)} %bitcast.21.x0.x1.x2.x3.xm.xo, bf16[4,1024,512]{2,1,0:T(8,128)(2,1)} %bitcast.21.x0.x1.x2.x3.xm.xo, bf16[4,1024,512]{2,1,0:T(8,128)(2,1)} %bitcast.21.x0.x1.x2.x3.xm.xo, ...), custom_call_target="tpu_custom_call" | custom-call | flops 48318384 | bytes 238551 | tf_op jit(solution)/shard_map/partial_x/pallas_call | solution.py:60
  123.0 5.0 %collective-permute-start.13 = (bf16[512,768]{1,0:T(8,128)(2,1)}, bf16[512,768]{1,0:T(8,128)(2,1)S(1)}, u32[]{:S(2)}, u32[]{:S(2)}) collective-permute-start(bf16[512,768]{1,0:T(8,128)(2,1)} %get-tuple-element.65), channel_id=1, source_target_pairs={{0,8},{8,0},{1,9},{9,1},{2,10},{10,2},{3,11},{11,3},{4,12},{12,4},... | collective-permute-start | bytes 2359304 | tf_op jit(solution)/shard_map/ppermute | solution.py:22
  132.6 6.0 %partial_c.2 = (bf16[512,384]{1,0:T(8,128)(2,1)}, f32[512,384]{1,0:T(8,128)}) custom-call(s32[1]{0:T(128)} %bitcast.3.places, bf16[4,1024,512]{2,1,0:T(8,128)(2,1)} %constant_dynamic-update-slice_fusion.5.cot.cm.co, bf16[2048,1152]{1,0:T(8,128)(2,1)} %all-gather.3.cloned.1.call-done.w.wa), custom_call_target="tpu_custom_call" | custom-call | flops 16106127 | bytes 100925 | tf_op jit(solution)/shard_map/partial_c/pallas_call | solution.py:60
  141.5 4.1 %activate.2.dm.ma = bf16[512,1152]{1,0:T(8,128)(2,1)} custom-call(s32[1]{0:T(128)} %bitcast.3.places, f32[512,768]{1,0:T(8,128)} %get-tuple-element.64.mine, bf16[512,768]{1,0:T(8,128)(2,1)} %copy-done.6, f32[512,384]{1,0:T(8,128)} %get-tuple-element.66.mine_d, bf16[512,384]{1,0:T(8,128)(2,1)} %copy-done.10), custom_call_target="tpu_custom_call" | custom-call | flops 58982 | bytes 47185 | tf_op jit(solution)/shard_map/activate/pallas_call | solution.py:60
  149.7 11.0 %grads.2 = bf16[2048,1152]{1,0:T(8,128)(2,1)} custom-call(s32[10]{0:T(128)} %stack.121.places, bf16[4,1024,512]{2,1,0:T(8,128)(2,1)} %bitcast.21.x0.x1.x2.x3.xm.xo, bf16[4,1024,512]{2,1,0:T(8,128)(2,1)} %bitcast.21.x0.x1.x2.x3.xm.xo, bf16[4,1024,512]{2,1,0:T(8,128)(2,1)} %constant_dynamic-update-slice_fusion.5.cot.cm.co, ...), custom_call_target="tpu_custom_call" | custom-call | flops 48318384 | bytes 238551 | tf_op jit(solution)/shard_map/grads/pallas_call | solution.py:60
  161.0 9.2 %partial_x.3 = (bf16[512,1024]{1,0:T(8,128)(2,1)}, f32[512,1024]{1,0:T(8,128)}) custom-call(s32[5]{0:T(128)} %stack.122.places, bf16[4,1024,512]{2,1,0:T(8,128)(2,1)} %bitcast.21.x0.x1.x2.x3.xm.xo, bf16[4,1024,512]{2,1,0:T(8,128)(2,1)} %bitcast.21.x0.x1.x2.x3.xm.xo, bf16[4,1024,512]{2,1,0:T(8,128)(2,1)} %bitcast.21.x0.x1.x2.x3.xm.xo, ...), custom_call_target="tpu_custom_call" | custom-call | flops 64424508 | bytes 262144 | tf_op jit(solution)/shard_map/partial_x/pallas_call | solution.py:60
  170.3 5.9 %partial_c.3 = (bf16[512,512]{1,0:T(8,128)(2,1)}, f32[512,512]{1,0:T(8,128)}) custom-call(s32[1]{0:T(128)} %bitcast.3.places, bf16[4,1024,512]{2,1,0:T(8,128)(2,1)} %constant_dynamic-update-slice_fusion.5.cot.cm.co, bf16[2048,1536]{1,0:T(8,128)(2,1)} %all-gather.5.cloned.1.call-done.w.wb), custom_call_target="tpu_custom_call" | custom-call | flops 21474836 | bytes 120586 | tf_op jit(solution)/shard_map/partial_c/pallas_call | solution.py:60
  179.6 4.4 %activate.3.mb.dm = bf16[512,1536]{1,0:T(8,128)(2,1)} custom-call(s32[1]{0:T(128)} %bitcast.3.places, f32[512,1024]{1,0:T(8,128)} %get-tuple-element.71.mine, bf16[512,1024]{1,0:T(8,128)(2,1)} %copy-done.5, f32[512,512]{1,0:T(8,128)} %get-tuple-element.73.mine_d, bf16[512,512]{1,0:T(8,128)(2,1)} %copy-done.9), custom_call_target="tpu_custom_call" | custom-call | flops 78643 | bytes 62914 | tf_op jit(solution)/shard_map/activate/pallas_call | solution.py:60
  185.0 2.7 collective-permute-done.18.ob.do
  188.8 7.3 %d_x.2 = bf16[1024,512]{1,0:T(8,128)(2,1)} custom-call(s32[2]{0:T(128)} %pad_add_fusion.1.places, bf16[2048,1152]{1,0:T(8,128)(2,1)} %all-gather.3.cloned.1.call-done.w.wa, bf16[2048,1536]{1,0:T(8,128)(2,1)} %all-gather.5.cloned.1.call-done.w.wb, bf16[512,1152]{1,0:T(8,128)(2,1)} %activate.2.dm.ma, bf16[512,1152]{1,0:T(8,128)(2,1)} %copy-done.1, ...), custom_call_target="tpu_custom_call" | custom-call | flops 18790480 | bytes 175636 | tf_op jit(solution)/shard_map/d_x/pallas_call | solution.py:60
  196.0 12.3 %grads.3 = bf16[2048,1536]{1,0:T(8,128)(2,1)} custom-call(s32[10]{0:T(128)} %stack.121.places, bf16[4,1024,512]{2,1,0:T(8,128)(2,1)} %bitcast.21.x0.x1.x2.x3.xm.xo, bf16[4,1024,512]{2,1,0:T(8,128)(2,1)} %bitcast.21.x0.x1.x2.x3.xm.xo, bf16[4,1024,512]{2,1,0:T(8,128)(2,1)} %constant_dynamic-update-slice_fusion.5.cot.cm.co, ...), custom_call_target="tpu_custom_call" | custom-call | flops 64424508 | bytes 262144 | tf_op jit(solution)/shard_map/grads/pallas_call | solution.py:60
  211.9 11.6 %d_x.3.terms = bf16[3072,512]{1,0:T(8,128)(2,1)} custom-call(s32[4]{0:T(128)} %pad_add_fusion.places, bf16[2048,1152]{1,0:T(8,128)(2,1)} %all-gather.3.cloned.1.call-done.w.wa, bf16[2048,1536]{1,0:T(8,128)(2,1)} %all-gather.5.cloned.1.call-done.w.wb, bf16[512,1152]{1,0:T(8,128)(2,1)} %activate.2.dm.ma, bf16[512,1152]{1,0:T(8,128)(2,1)} %copy-done.1, ...), custom_call_target="tpu_custom_call" | custom-call | flops 56371444 | bytes 196608 | tf_op jit(solution)/shard_map/d_x/pallas_call | solution.py:60
  226.3 3.3 %merge.1 = (bf16[1024,512]{1,0:T(8,128)(2,1)}, bf16[1024,512]{1,0:T(8,128)(2,1)}) custom-call(s32[1]{0:T(128)} %constant.121.clone.1.places, bf16[3072,512]{1,0:T(8,128)(2,1)} %d_x.3.terms, bf16[512,512]{1,0:T(8,128)(2,1)} %copy-done.8, bf16[512,512]{1,0:T(8,128)(2,1)} %copy-done.7), custom_call_target="tpu_custom_call" | custom-call | bytes 62914 | tf_op jit(solution)/shard_map/merge/pallas_call | solution.py:60
  229.7 2.7 collective-permute-start.22
  235.3 19.3 %collective-permute-done.21 = bf16[1024,512]{1,0:T(8,128)(2,1)S(1)} collective-permute-done((bf16[1024,512]{1,0:T(8,128)(2,1)}, bf16[1024,512]{1,0:T(8,128)(2,1)S(1)}, u32[]{:S(2)}, u32[]{:S(2)}) %collective-permute-start.21) | collective-permute-done | bytes 1048608 | tf_op jit(solution)/shard_map/ppermute | solution.py:18
  257.9 2.6 collective-permute-start.25
  260.5 3.2 %collective-permute-done.26 = bf16[512,256]{1,0:T(8,128)(2,1)S(1)} collective-permute-done((bf16[512,256]{1,0:T(8,128)(2,1)S(1)}, bf16[512,256]{1,0:T(8,128)(2,1)S(1)}, u32[]{:S(2)}, u32[]{:S(2)}) %collective-permute-start.26) | collective-permute-done | bytes 262176 | tf_op jit(solution)/shard_map/ppermute | solution.py:26
  263.7 7.6 %collective-permute-done.25 = bf16[512,256]{1,0:T(8,128)(2,1)S(1)} collective-permute-done((bf16[512,256]{1,0:T(8,128)(2,1)S(1)}, bf16[512,256]{1,0:T(8,128)(2,1)S(1)}, u32[]{:S(2)}, u32[]{:S(2)}) %collective-permute-start.25) | collective-permute-done | bytes 262176 | tf_op jit(solution)/shard_map/ppermute | solution.py:34
  277.2 2.8 collective-permute-start.28
  280.0 17.2 %collective-permute-done.28 = bf16[256,1536]{1,0:T(8,128)(2,1)S(1)} collective-permute-done((bf16[256,1536]{1,0:T(8,128)(2,1)S(1)}, bf16[256,1536]{1,0:T(8,128)(2,1)S(1)}, u32[]{:S(2)}, u32[]{:S(2)}) %collective-permute-start.28) | collective-permute-done | bytes 786464 | tf_op jit(solution)/shard_map/ppermute | solution.py:26
  (151 shorter events, 68.9 us)
Async XLA Ops:
  7.2 106.7 %all-gather.3.cloned.1.call-start = ((), (), s32[]{:S(2)}) async-start(), calls=%async_computation.2 | async-start | bytes 5898240 | tf_op jit(solution)/shard_map/all_gather | solution.py:242
  8.7 3.1 %collective-permute-start = (bf16[256,1152]{1,0:T(8,128)(2,1)S(1)}, bf16[256,1152]{1,0:T(8,128)(2,1)S(1)}, u32[]{:S(2)}, u32[]{:S(2)}) collective-permute-start(bf16[256,1152]{1,0:T(8,128)(2,1)S(1)} %pad_maximum_fusion.9), channel_id=1, source_target_pairs={{0,8},{8,0},{1,9},{9,1},{2,10},{10,2},{3,11},{11,3},{4,12},{12,4},... | collective-permute-start | bytes 1769480 | tf_op jit(solution)/shard_map/ppermute | solution.py:22
  12.0 16.7 %collective-permute-start.1 = (bf16[256,1152]{1,0:T(8,128)(2,1)S(1)}, bf16[256,1152]{1,0:T(8,128)(2,1)S(1)}, u32[]{:S(2)}, u32[]{:S(2)}) collective-permute-start(bf16[256,1152]{1,0:T(8,128)(2,1)S(1)} %get-tuple-element.111), channel_id=1, source_target_pairs={{0,1},{1,0},{2,3},{3,2},{4,5},{5,4},{6,7},{7,6},{8,9},{9,8},{10,11... | collective-permute-start | bytes 1769480 | tf_op jit(solution)/shard_map/ppermute | solution.py:26
  29.9 131.1 %all-gather.5.cloned.1.call-start = ((), (), s32[]{:S(2)}) async-start(), calls=%async_computation.3 | async-start | bytes 7864320 | tf_op jit(solution)/shard_map/all_gather | solution.py:257
  32.4 18.3 %collective-permute-start.5 = (bf16[256,1536]{1,0:T(8,128)(2,1)S(1)}, bf16[256,1536]{1,0:T(8,128)(2,1)S(1)}, u32[]{:S(2)}, u32[]{:S(2)}) collective-permute-start(bf16[256,1536]{1,0:T(8,128)(2,1)S(1)} %pad_maximum_fusion.7), channel_id=1, source_target_pairs={{0,8},{8,0},{1,9},{9,1},{2,10},{10,2},{3,11},{11,3},{4,12},{12,4},... | collective-permute-start | bytes 2359304 | tf_op jit(solution)/shard_map/ppermute | solution.py:22
  33.2 7.2 %collective-permute-start.2 = (bf16[512,256]{1,0:T(8,128)(2,1)S(1)}, bf16[512,256]{1,0:T(8,128)(2,1)S(1)}, u32[]{:S(2)}, u32[]{:S(2)}) collective-permute-start(bf16[512,256]{1,0:T(8,128)(2,1)S(1)} %copy-done.11), channel_id=1, source_target_pairs={{0,16},{16,0},{1,17},{17,1},{2,18},{18,2},{3,19},{19,3},{4,20},{20... | collective-permute-start | bytes 786440 | tf_op jit(solution)/shard_map/ppermute | solution.py:30
  34.4 13.9 %collective-permute-start.3 = (bf16[512,256]{1,0:T(8,128)(2,1)S(1)}, bf16[512,256]{1,0:T(8,128)(2,1)S(1)}, u32[]{:S(2)}, u32[]{:S(2)}) collective-permute-start(bf16[512,256]{1,0:T(8,128)(2,1)S(1)} %copy-done.11), channel_id=1, source_target_pairs={{0,1},{1,0},{2,3},{3,2},{4,5},{5,4},{6,7},{7,6},{8,9},{9,8},{10,11... | collective-permute-start | bytes 786440 | tf_op jit(solution)/shard_map/ppermute | solution.py:26
  37.0 13.5 %collective-permute-start.4 = (bf16[512,256]{1,0:T(8,128)(2,1)S(1)}, bf16[512,256]{1,0:T(8,128)(2,1)S(1)}, u32[]{:S(2)}, u32[]{:S(2)}) collective-permute-start(bf16[512,256]{1,0:T(8,128)(2,1)S(1)} %copy-done.11), channel_id=1, source_target_pairs={{0,17},{17,0},{1,16},{16,1},{2,19},{19,2},{3,18},{18,3},{4,21},{21... | collective-permute-start | bytes 786440 | tf_op jit(solution)/shard_map/ppermute | solution.py:34
  51.0 18.5 %collective-permute-start.6 = (bf16[256,1536]{1,0:T(8,128)(2,1)S(1)}, bf16[256,1536]{1,0:T(8,128)(2,1)S(1)}, u32[]{:S(2)}, u32[]{:S(2)}) collective-permute-start(bf16[256,1536]{1,0:T(8,128)(2,1)S(1)} %get-tuple-element.56), channel_id=1, source_target_pairs={{0,1},{1,0},{2,3},{3,2},{4,5},{5,4},{6,7},{7,6},{8,9},{9,8},{10,11... | collective-permute-start | bytes 2359304 | tf_op jit(solution)/shard_map/ppermute | solution.py:26
  70.9 161.5 %reduce-scatter.3.cloned.1.call-start = ((), (), s32[]{:S(2)}) async-start(), calls=%async_computation.4 | async-start | bytes 5898240 | tf_op jit(solution)/shard_map/reduce_scatter | solution.py:269
  70.9 23.3 %collective-permute-start.8 = (bf16[1024,512]{1,0:T(8,128)(2,1)S(1)}, bf16[1024,512]{1,0:T(8,128)(2,1)S(1)}, u32[]{:S(2)}, u32[]{:S(2)}) collective-permute-start(bf16[1024,512]{1,0:T(8,128)(2,1)S(1)} %pad_maximum_fusion.2), channel_id=1, source_target_pairs={{0,96},{32,0},{64,32},{96,64},{1,97},{33,1},{65,33},{97,65},{2,98}... | collective-permute-start | bytes 3145736 | tf_op jit(solution)/shard_map/ppermute | solution.py:18
  74.7 22.7 %collective-permute-start.7 = (bf16[1024,512]{1,0:T(8,128)(2,1)S(1)}, bf16[1024,512]{1,0:T(8,128)(2,1)S(1)}, u32[]{:S(2)}, u32[]{:S(2)}) collective-permute-start(bf16[1024,512]{1,0:T(8,128)(2,1)S(1)} %pad_maximum_fusion.2), channel_id=1, source_target_pairs={{0,32},{32,64},{64,96},{96,0},{1,33},{33,65},{65,97},{97,1},{2,34}... | collective-permute-start | bytes 3145736 | tf_op jit(solution)/shard_map/ppermute | solution.py:18
  74.7 23.5 %collective-permute-start.11 = (bf16[4,256,512]{2,1,0:T(8,128)(2,1)}, bf16[4,256,512]{2,1,0:T(8,128)(2,1)}, u32[]{:S(2)}, u32[]{:S(2)}) collective-permute-start(bf16[4,256,512]{2,1,0:T(8,128)(2,1)} %columns.3), channel_id=1, source_target_pairs={{0,17},{17,0},{1,16},{16,1},{2,19},{19,2},{3,18},{18,3},{4,21},{21... | collective-permute-start | bytes 3145736 | tf_op jit(solution)/shard_map/ppermute | solution.py:34
  98.2 10.8 %collective-permute-start.9 = (bf16[512,512]{1,0:T(8,128)(2,1)}, bf16[512,512]{1,0:T(8,128)(2,1)}, u32[]{:S(2)}, u32[]{:S(2)}) collective-permute-start(bf16[512,512]{1,0:T(8,128)(2,1)} %slice.96), channel_id=1, source_target_pairs={{0,32},{32,64},{64,96},{96,0},{1,33},{33,65},{65,97},{97,1},{2,34}... | collective-permute-start | bytes 1572872 | tf_op jit(solution)/shard_map/ppermute | solution.py:18
  98.2 32.1 %collective-permute-start.12 = (bf16[4,256,512]{2,1,0:T(8,128)(2,1)}, bf16[4,256,512]{2,1,0:T(8,128)(2,1)}, u32[]{:S(2)}, u32[]{:S(2)}) collective-permute-start(bf16[4,256,512]{2,1,0:T(8,128)(2,1)} %collective-permute-done.11), channel_id=1, source_target_pairs={{0,16},{16,0},{1,17},{17,1},{2,18},{18,2},{3,19},{19,3},{4,20},{20... | collective-permute-start | bytes 3145736 | tf_op jit(solution)/shard_map/ppermute | solution.py:30
  99.1 11.9 %collective-permute-start.10 = (bf16[512,512]{1,0:T(8,128)(2,1)}, bf16[512,512]{1,0:T(8,128)(2,1)}, u32[]{:S(2)}, u32[]{:S(2)}) collective-permute-start(bf16[512,512]{1,0:T(8,128)(2,1)} %slice.97), channel_id=1, source_target_pairs={{0,96},{32,0},{64,32},{96,64},{1,97},{33,1},{65,33},{97,65},{2,98}... | collective-permute-start | bytes 1572872 | tf_op jit(solution)/shard_map/ppermute | solution.py:18
  123.0 17.5 %collective-permute-start.13 = (bf16[512,768]{1,0:T(8,128)(2,1)}, bf16[512,768]{1,0:T(8,128)(2,1)S(1)}, u32[]{:S(2)}, u32[]{:S(2)}) collective-permute-start(bf16[512,768]{1,0:T(8,128)(2,1)} %get-tuple-element.65), channel_id=1, source_target_pairs={{0,8},{8,0},{1,9},{9,1},{2,10},{10,2},{3,11},{11,3},{4,12},{12,4},... | collective-permute-start | bytes 2359304 | tf_op jit(solution)/shard_map/ppermute | solution.py:22
  145.6 3.1 collective-permute-start.15
  160.7 115.2 %reduce-scatter.5.cloned.1.call-start = ((), (), s32[]{:S(2)}) async-start(), calls=%async_computation.5 | async-start | bytes 7864320 | tf_op jit(solution)/shard_map/reduce_scatter | solution.py:278
  170.2 8.2 %collective-permute-start.16 = (bf16[512,1024]{1,0:T(8,128)(2,1)}, bf16[512,1024]{1,0:T(8,128)(2,1)S(1)}, u32[]{:S(2)}, u32[]{:S(2)}) collective-permute-start(bf16[512,1024]{1,0:T(8,128)(2,1)} %get-tuple-element.72), channel_id=1, source_target_pairs={{0,8},{8,0},{1,9},{9,1},{2,10},{10,2},{3,11},{11,3},{4,12},{12,4},... | collective-permute-start | bytes 3145736 | tf_op jit(solution)/shard_map/ppermute | solution.py:22
  184.0 3.7 %collective-permute-start.18 = (bf16[512,1536]{1,0:T(8,128)(2,1)}, bf16[512,1536]{1,0:T(8,128)(2,1)S(1)}, u32[]{:S(2)}, u32[]{:S(2)}) collective-permute-start(bf16[512,1536]{1,0:T(8,128)(2,1)} %activate.3.mb.dm), channel_id=1, source_target_pairs={{0,8},{8,0},{1,9},{9,1},{2,10},{10,2},{3,11},{11,3},{4,12},{12,4},... | collective-permute-start | bytes 4718600 | tf_op jit(solution)/shard_map/ppermute | solution.py:22
  209.6 13.8 %collective-permute-start.20 = (bf16[512,512]{1,0:T(8,128)(2,1)S(1)}, bf16[512,512]{1,0:T(8,128)(2,1)S(1)}, u32[]{:S(2)}, u32[]{:S(2)}) collective-permute-start(bf16[512,512]{1,0:T(8,128)(2,1)S(1)} %get-tuple-element.112), channel_id=1, source_target_pairs={{0,96},{32,0},{64,32},{96,64},{1,97},{33,1},{65,33},{97,65},{2,98}... | collective-permute-start | bytes 1572872 | tf_op jit(solution)/shard_map/ppermute | solution.py:18
  211.3 14.2 %collective-permute-start.19 = (bf16[512,512]{1,0:T(8,128)(2,1)S(1)}, bf16[512,512]{1,0:T(8,128)(2,1)S(1)}, u32[]{:S(2)}, u32[]{:S(2)}) collective-permute-start(bf16[512,512]{1,0:T(8,128)(2,1)S(1)} %get-tuple-element.113), channel_id=1, source_target_pairs={{0,32},{32,64},{64,96},{96,0},{1,33},{33,65},{65,97},{97,1},{2,34}... | collective-permute-start | bytes 1572872 | tf_op jit(solution)/shard_map/ppermute | solution.py:18
  229.6 24.9 %collective-permute-start.21 = (bf16[1024,512]{1,0:T(8,128)(2,1)}, bf16[1024,512]{1,0:T(8,128)(2,1)S(1)}, u32[]{:S(2)}, u32[]{:S(2)}) collective-permute-start(bf16[1024,512]{1,0:T(8,128)(2,1)} %get-tuple-element.81), channel_id=1, source_target_pairs={{0,32},{32,64},{64,96},{96,0},{1,33},{33,65},{65,97},{97,1},{2,34}... | collective-permute-start | bytes 3145736 | tf_op jit(solution)/shard_map/ppermute | solution.py:18
  229.7 24.9 %collective-permute-start.22 = (bf16[1024,512]{1,0:T(8,128)(2,1)}, bf16[1024,512]{1,0:T(8,128)(2,1)S(1)}, u32[]{:S(2)}, u32[]{:S(2)}) collective-permute-start(bf16[1024,512]{1,0:T(8,128)(2,1)} %get-tuple-element.82), channel_id=1, source_target_pairs={{0,96},{32,0},{64,32},{96,64},{1,97},{33,1},{65,33},{97,65},{2,98}... | collective-permute-start | bytes 3145736 | tf_op jit(solution)/shard_map/ppermute | solution.py:18
  233.7 20.9 %collective-permute-start.23 = (bf16[256,1152]{1,0:T(8,128)(2,1)S(1)}, bf16[256,1152]{1,0:T(8,128)(2,1)S(1)}, u32[]{:S(2)}, u32[]{:S(2)}) collective-permute-start(bf16[256,1152]{1,0:T(8,128)(2,1)S(1)} %get-tuple-element.109), channel_id=1, source_target_pairs={{0,1},{1,0},{2,3},{3,2},{4,5},{5,4},{6,7},{7,6},{8,9},{9,8},{10,11... | collective-permute-start | bytes 1769480 | tf_op jit(solution)/shard_map/ppermute | solution.py:26
  256.4 7.3 %collective-permute-start.26 = (bf16[512,256]{1,0:T(8,128)(2,1)S(1)}, bf16[512,256]{1,0:T(8,128)(2,1)S(1)}, u32[]{:S(2)}, u32[]{:S(2)}) collective-permute-start(bf16[512,256]{1,0:T(8,128)(2,1)S(1)} %slice.152), channel_id=1, source_target_pairs={{0,1},{1,0},{2,3},{3,2},{4,5},{5,4},{6,7},{7,6},{8,9},{9,8},{10,11... | collective-permute-start | bytes 786440 | tf_op jit(solution)/shard_map/ppermute | solution.py:26
  257.9 13.4 %collective-permute-start.25 = (bf16[512,256]{1,0:T(8,128)(2,1)S(1)}, bf16[512,256]{1,0:T(8,128)(2,1)S(1)}, u32[]{:S(2)}, u32[]{:S(2)}) collective-permute-start(bf16[512,256]{1,0:T(8,128)(2,1)S(1)} %get-tuple-element.114), channel_id=1, source_target_pairs={{0,17},{17,0},{1,16},{16,1},{2,19},{19,2},{3,18},{18,3},{4,21},{21... | collective-permute-start | bytes 786440 | tf_op jit(solution)/shard_map/ppermute | solution.py:34
  260.5 10.8 %collective-permute-start.24 = (bf16[512,256]{1,0:T(8,128)(2,1)S(1)}, bf16[512,256]{1,0:T(8,128)(2,1)S(1)}, u32[]{:S(2)}, u32[]{:S(2)}) collective-permute-start(bf16[512,256]{1,0:T(8,128)(2,1)S(1)} %get-tuple-element.115), channel_id=1, source_target_pairs={{0,16},{16,0},{1,17},{17,1},{2,18},{18,2},{3,19},{19,3},{4,20},{20... | collective-permute-start | bytes 786440 | tf_op jit(solution)/shard_map/ppermute | solution.py:30
  272.1 2.7 collective-permute-start.27
  277.2 20.1 %collective-permute-start.28 = (bf16[256,1536]{1,0:T(8,128)(2,1)S(1)}, bf16[256,1536]{1,0:T(8,128)(2,1)S(1)}, u32[]{:S(2)}, u32[]{:S(2)}) collective-permute-start(bf16[256,1536]{1,0:T(8,128)(2,1)S(1)} %slice.111), channel_id=1, source_target_pairs={{0,1},{1,0},{2,3},{3,2},{4,5},{5,4},{6,7},{7,6},{8,9},{9,8},{10,11... | collective-permute-start | bytes 2359304 | tf_op jit(solution)/shard_map/ppermute | solution.py:26
  297.4 3.5 %collective-permute-start.29 = (bf16[256,1536]{1,0:T(8,128)(2,1)S(1)}, bf16[256,1536]{1,0:T(8,128)(2,1)S(1)}, u32[]{:S(2)}, u32[]{:S(2)}) collective-permute-start(bf16[256,1536]{1,0:T(8,128)(2,1)S(1)} %get-tuple-element.97), channel_id=1, source_target_pairs={{0,8},{8,0},{1,9},{9,1},{2,10},{10,2},{3,11},{11,3},{4,12},{12,4},... | collective-permute-start | bytes 2359304 | tf_op jit(solution)/shard_map/ppermute | solution.py:22
  (25 other events, 57.4 us)
Sparse Core Ops, SparseCore 0:
  30.0 54.9 all-gather.2
  86.7 66.0 all-gather.4
  160.8 49.0 reduce-scatter.2
  212.2 63.6 reduce-scatter.4

commit v4 on v3

--- a/solution.py
+++ b/solution.py
@@ -255,8 +255,9 @@
     X = cat(here, z_after, up, down, z_before).reshape(4, pair, block)
 
     WB = lax.all_gather(ownB, "x", axis=0, tiled=True)
-    for i, v in ((yl, part), (1 - yl, rest)):
-        C = lax.dynamic_update_slice_in_dim(C, v, rows + i * half, 1)
+    C = lax.dynamic_update_slice_in_dim(C, part, rows + yl * half, 1)
+    X, C = after((X, C))
+    C = lax.dynamic_update_slice_in_dim(C, rest, rows + (1 - yl) * half, 1)
 
     def compute(W):
         theirs, mine = partial_x(X, W, places)

time: 313 us -> 312 us (level)
  no operation moved by 1% of the time
where the time goes in v4:
time: 312 us; the launch traced here: 311 us
  waiting for transfers between devices  123 us (39%)
  Pallas kernels  96.6 us (31%)
  starting transfers between devices  35.7 us (11%)
  local copies, waits for them, and re-layouts  31.1 us (10%)
  between operations  14.1 us (5%)
  other arithmetic  10.5 us (3%)
    pallas_call x13, Pallas kernels, call(): pl.pallas_call(body, grid_spec=pltpu.PrefetchScalarGridSpec(num_scalar_pr...  96.6 us
    ppermute x8, waiting for transfers between devices, ring(): return lax.ppermute(v, axis, [(i, (i + step) % 4) for i in range(4)])  48.6 us
    ppermute x6, waiting for transfers between devices, across(): return lax.ppermute(v, 'yh', SWAP)  47.8 us
    unnamed x43, local copies, waits for them, and re-layouts  15.8 us
    ppermute x10, waiting for transfers between devices, sibling(): return lax.ppermute(v, 'c', SWAP)  12.7 us
    ppermute x8, starting transfers between devices, ring(): return lax.ppermute(v, axis, [(i, (i + step) % 4) for i in range(4)])  10.9 us
    ppermute x10, starting transfers between devices, sibling(): return lax.ppermute(v, 'c', SWAP)  10.8 us
    ppermute x6, starting transfers between devices, across(): return lax.ppermute(v, 'yh', SWAP)  10.4 us
  transfers between devices with their start and end apart: 34, of which 20 were waited for; matrix products, arithmetic and copies ran while one was open for 8% of the time, Pallas kernels for 31%

profile of v4, /device:TPU:1, one launch (start us, length us, event | category | flops | bytes accessed | tf_op | source)
XLA Modules:
  0.0 310.8 jit_solution(13986531160813297834)
XLA Ops:
  12.0 3.1 collective-permute-start.1
  16.4 5.9 %columns.3 = bf16[4,256,512]{2,1,0:T(8,128)(2,1)} custom-call(s32[9]{0:T(128)} %concatenate.67.places, bf16[512,4096]{1,0:T(8,128)(2,1)} %src.1), custom_call_target="tpu_custom_call" | custom-call | bytes 52428 | tf_op jit(solution)/shard_map/columns/pallas_call | solution.py:60
  22.4 6.4 %columns.2 = bf16[4,1024,512]{2,1,0:T(8,128)(2,1)} custom-call(s32[9]{0:T(128)} %concatenate.66.places, bf16[512,4096]{1,0:T(8,128)(2,1)} %src.1), custom_call_target="tpu_custom_call" | custom-call | bytes 83886 | tf_op jit(solution)/shard_map/columns/pallas_call | solution.py:60
  34.4 2.6 collective-permute-start.3
  37.0 3.3 %collective-permute-done.2 = bf16[512,256]{1,0:T(8,128)(2,1)S(1)} collective-permute-done((bf16[512,256]{1,0:T(8,128)(2,1)S(1)}, bf16[512,256]{1,0:T(8,128)(2,1)S(1)}, u32[]{:S(2)}, u32[]{:S(2)}) %collective-permute-start.2) | collective-permute-done | bytes 262176 | tf_op jit(solution)/shard_map/ppermute | solution.py:30
  40.5 7.8 %collective-permute-done.3 = bf16[512,256]{1,0:T(8,128)(2,1)S(1)} collective-permute-done((bf16[512,256]{1,0:T(8,128)(2,1)S(1)}, bf16[512,256]{1,0:T(8,128)(2,1)S(1)}, u32[]{:S(2)}, u32[]{:S(2)}) %collective-permute-start.3) | collective-permute-done | bytes 262176 | tf_op jit(solution)/shard_map/ppermute | solution.py:26
  51.1 18.4 %collective-permute-done.6 = bf16[256,1536]{1,0:T(8,128)(2,1)S(1)} collective-permute-done((bf16[256,1536]{1,0:T(8,128)(2,1)S(1)}, bf16[256,1536]{1,0:T(8,128)(2,1)S(1)}, u32[]{:S(2)}, u32[]{:S(2)}) %collective-permute-start.6) | collective-permute-done | bytes 786464 | tf_op jit(solution)/shard_map/ppermute | solution.py:26
  70.9 3.8 %collective-permute-start.8 = (bf16[1024,512]{1,0:T(8,128)(2,1)S(1)}, bf16[1024,512]{1,0:T(8,128)(2,1)S(1)}, u32[]{:S(2)}, u32[]{:S(2)}) collective-permute-start(bf16[1024,512]{1,0:T(8,128)(2,1)S(1)} %pad_maximum_fusion.2), channel_id=1, source_target_pairs={{0,96},{32,0},{64,32},{96,64},{1,97},{33,1},{65,33},{97,65},{2,98}... | collective-permute-start | bytes 3145736 | tf_op jit(solution)/shard_map/ppermute | solution.py:18
  74.8 19.3 %collective-permute-done.8 = bf16[1024,512]{1,0:T(8,128)(2,1)S(1)} collective-permute-done((bf16[1024,512]{1,0:T(8,128)(2,1)S(1)}, bf16[1024,512]{1,0:T(8,128)(2,1)S(1)}, u32[]{:S(2)}, u32[]{:S(2)}) %collective-permute-start.8) | collective-permute-done | bytes 1048608 | tf_op jit(solution)/shard_map/ppermute | solution.py:18
  94.2 3.2 %collective-permute-done.7 = bf16[1024,512]{1,0:T(8,128)(2,1)S(1)} collective-permute-done((bf16[1024,512]{1,0:T(8,128)(2,1)S(1)}, bf16[1024,512]{1,0:T(8,128)(2,1)S(1)}, u32[]{:S(2)}, u32[]{:S(2)}) %collective-permute-start.7) | collective-permute-done | bytes 1048608 | tf_op jit(solution)/shard_map/ppermute | solution.py:18
  99.1 2.7 collective-permute-start.10
  104.5 4.6 %collective-permute-done.9 = bf16[512,512]{1,0:T(8,128)(2,1)} collective-permute-done((bf16[512,512]{1,0:T(8,128)(2,1)}, bf16[512,512]{1,0:T(8,128)(2,1)}, u32[]{:S(2)}, u32[]{:S(2)}) %collective-permute-start.9) | collective-permute-done | bytes 524320 | tf_op jit(solution)/shard_map/ppermute | solution.py:18
  116.2 9.0 %partial_x.2 = (bf16[512,768]{1,0:T(8,128)(2,1)}, f32[512,768]{1,0:T(8,128)}) custom-call(s32[5]{0:T(128)} %stack.122.places, bf16[4,1024,512]{2,1,0:T(8,128)(2,1)} %bitcast.21.x0.x1.x2.x3.xm.xo, bf16[4,1024,512]{2,1,0:T(8,128)(2,1)} %bitcast.21.x0.x1.x2.x3.xm.xo, bf16[4,1024,512]{2,1,0:T(8,128)(2,1)} %bitcast.21.x0.x1.x2.x3.xm.xo, ...), custom_call_target="tpu_custom_call" | custom-call | flops 48318384 | bytes 238551 | tf_op jit(solution)/shard_map/partial_x/pallas_call | solution.py:60
  125.2 5.0 %collective-permute-start.13 = (bf16[512,768]{1,0:T(8,128)(2,1)}, bf16[512,768]{1,0:T(8,128)(2,1)S(1)}, u32[]{:S(2)}, u32[]{:S(2)}) collective-permute-start(bf16[512,768]{1,0:T(8,128)(2,1)} %get-tuple-element.69), channel_id=1, source_target_pairs={{0,8},{8,0},{1,9},{9,1},{2,10},{10,2},{3,11},{11,3},{4,12},{12,4},... | collective-permute-start | bytes 2359304 | tf_op jit(solution)/shard_map/ppermute | solution.py:22
  132.5 6.0 %partial_c.2 = (bf16[512,384]{1,0:T(8,128)(2,1)}, f32[512,384]{1,0:T(8,128)}) custom-call(s32[1]{0:T(128)} %bitcast.3.places, bf16[4,1024,512]{2,1,0:T(8,128)(2,1)} %constant_dynamic-update-slice_fusion.5.cot.cm.co, bf16[2048,1152]{1,0:T(8,128)(2,1)} %all-gather.3.cloned.1.call-done.w.wa), custom_call_target="tpu_custom_call" | custom-call | flops 16106127 | bytes 100925 | tf_op jit(solution)/shard_map/partial_c/pallas_call | solution.py:60
  141.4 4.1 %activate.2.dm.ma = bf16[512,1152]{1,0:T(8,128)(2,1)} custom-call(s32[1]{0:T(128)} %bitcast.3.places, f32[512,768]{1,0:T(8,128)} %get-tuple-element.68.mine, bf16[512,768]{1,0:T(8,128)(2,1)} %copy-done.6, f32[512,384]{1,0:T(8,128)} %get-tuple-element.70.mine_d, bf16[512,384]{1,0:T(8,128)(2,1)} %copy-done.10), custom_call_target="tpu_custom_call" | custom-call | flops 58982 | bytes 47185 | tf_op jit(solution)/shard_map/activate/pallas_call | solution.py:60
  146.3 2.3 collective-permute-done.15.do.oa
  149.6 11.0 %grads.2 = bf16[2048,1152]{1,0:T(8,128)(2,1)} custom-call(s32[10]{0:T(128)} %stack.121.places, bf16[4,1024,512]{2,1,0:T(8,128)(2,1)} %bitcast.21.x0.x1.x2.x3.xm.xo, bf16[4,1024,512]{2,1,0:T(8,128)(2,1)} %bitcast.21.x0.x1.x2.x3.xm.xo, bf16[4,1024,512]{2,1,0:T(8,128)(2,1)} %constant_dynamic-update-slice_fusion.5.cot.cm.co, ...), custom_call_target="tpu_custom_call" | custom-call | flops 48318384 | bytes 238551 | tf_op jit(solution)/shard_map/grads/pallas_call | solution.py:60
  160.9 9.2 %partial_x.3 = (bf16[512,1024]{1,0:T(8,128)(2,1)}, f32[512,1024]{1,0:T(8,128)}) custom-call(s32[5]{0:T(128)} %stack.122.places, bf16[4,1024,512]{2,1,0:T(8,128)(2,1)} %bitcast.21.x0.x1.x2.x3.xm.xo, bf16[4,1024,512]{2,1,0:T(8,128)(2,1)} %bitcast.21.x0.x1.x2.x3.xm.xo, bf16[4,1024,512]{2,1,0:T(8,128)(2,1)} %bitcast.21.x0.x1.x2.x3.xm.xo, ...), custom_call_target="tpu_custom_call" | custom-call | flops 64424508 | bytes 262144 | tf_op jit(solution)/shard_map/partial_x/pallas_call | solution.py:60
  170.2 5.9 %partial_c.3 = (bf16[512,512]{1,0:T(8,128)(2,1)}, f32[512,512]{1,0:T(8,128)}) custom-call(s32[1]{0:T(128)} %bitcast.3.places, bf16[4,1024,512]{2,1,0:T(8,128)(2,1)} %constant_dynamic-update-slice_fusion.5.cot.cm.co, bf16[2048,1536]{1,0:T(8,128)(2,1)} %all-gather.5.cloned.1.call-done.w.wb), custom_call_target="tpu_custom_call" | custom-call | flops 21474836 | bytes 120586 | tf_op jit(solution)/shard_map/partial_c/pallas_call | solution.py:60
  179.5 4.4 %activate.3.mb.dm = bf16[512,1536]{1,0:T(8,128)(2,1)} custom-call(s32[1]{0:T(128)} %bitcast.3.places, f32[512,1024]{1,0:T(8,128)} %get-tuple-element.75.mine, bf16[512,1024]{1,0:T(8,128)(2,1)} %copy-done.5, f32[512,512]{1,0:T(8,128)} %get-tuple-element.77.mine_d, bf16[512,512]{1,0:T(8,128)(2,1)} %copy-done.9), custom_call_target="tpu_custom_call" | custom-call | flops 78643 | bytes 62914 | tf_op jit(solution)/shard_map/activate/pallas_call | solution.py:60
  184.8 2.7 collective-permute-done.18.ob.do
  188.7 7.2 %d_x.2 = bf16[1024,512]{1,0:T(8,128)(2,1)} custom-call(s32[2]{0:T(128)} %pad_add_fusion.1.places, bf16[2048,1152]{1,0:T(8,128)(2,1)} %all-gather.3.cloned.1.call-done.w.wa, bf16[2048,1536]{1,0:T(8,128)(2,1)} %all-gather.5.cloned.1.call-done.w.wb, bf16[512,1152]{1,0:T(8,128)(2,1)} %activate.2.dm.ma, bf16[512,1152]{1,0:T(8,128)(2,1)} %copy-done.1, ...), custom_call_target="tpu_custom_call" | custom-call | flops 18790480 | bytes 175636 | tf_op jit(solution)/shard_map/d_x/pallas_call | solution.py:60
  195.9 12.3 %grads.3 = bf16[2048,1536]{1,0:T(8,128)(2,1)} custom-call(s32[10]{0:T(128)} %stack.121.places, bf16[4,1024,512]{2,1,0:T(8,128)(2,1)} %bitcast.21.x0.x1.x2.x3.xm.xo, bf16[4,1024,512]{2,1,0:T(8,128)(2,1)} %bitcast.21.x0.x1.x2.x3.xm.xo, bf16[4,1024,512]{2,1,0:T(8,128)(2,1)} %constant_dynamic-update-slice_fusion.5.cot.cm.co, ...), custom_call_target="tpu_custom_call" | custom-call | flops 64424508 | bytes 262144 | tf_op jit(solution)/shard_map/grads/pallas_call | solution.py:60
  211.9 11.8 %d_x.3.terms = bf16[3072,512]{1,0:T(8,128)(2,1)} custom-call(s32[4]{0:T(128)} %pad_add_fusion.places, bf16[2048,1152]{1,0:T(8,128)(2,1)} %all-gather.3.cloned.1.call-done.w.wa, bf16[2048,1536]{1,0:T(8,128)(2,1)} %all-gather.5.cloned.1.call-done.w.wb, bf16[512,1152]{1,0:T(8,128)(2,1)} %activate.2.dm.ma, bf16[512,1152]{1,0:T(8,128)(2,1)} %copy-done.1, ...), custom_call_target="tpu_custom_call" | custom-call | flops 56371444 | bytes 196608 | tf_op jit(solution)/shard_map/d_x/pallas_call | solution.py:60
  226.2 3.3 %merge.1 = (bf16[1024,512]{1,0:T(8,128)(2,1)}, bf16[1024,512]{1,0:T(8,128)(2,1)}) custom-call(s32[1]{0:T(128)} %constant.121.clone.1.places, bf16[3072,512]{1,0:T(8,128)(2,1)} %d_x.3.terms, bf16[512,512]{1,0:T(8,128)(2,1)} %copy-done.8, bf16[512,512]{1,0:T(8,128)(2,1)} %copy-done.7), custom_call_target="tpu_custom_call" | custom-call | bytes 62914 | tf_op jit(solution)/shard_map/merge/pallas_call | solution.py:60
  229.5 2.7 collective-permute-start.22
  234.5 19.7 %collective-permute-done.21 = bf16[1024,512]{1,0:T(8,128)(2,1)S(1)} collective-permute-done((bf16[1024,512]{1,0:T(8,128)(2,1)}, bf16[1024,512]{1,0:T(8,128)(2,1)S(1)}, u32[]{:S(2)}, u32[]{:S(2)}) %collective-permute-start.21) | collective-permute-done | bytes 1048608 | tf_op jit(solution)/shard_map/ppermute | solution.py:18
  259.1 4.3 %collective-permute-done.26 = bf16[512,256]{1,0:T(8,128)(2,1)S(1)} collective-permute-done((bf16[512,256]{1,0:T(8,128)(2,1)S(1)}, bf16[512,256]{1,0:T(8,128)(2,1)S(1)}, u32[]{:S(2)}, u32[]{:S(2)}) %collective-permute-start.26) | collective-permute-done | bytes 262176 | tf_op jit(solution)/shard_map/ppermute | solution.py:26
  263.3 7.8 %collective-permute-done.25 = bf16[512,256]{1,0:T(8,128)(2,1)S(1)} collective-permute-done((bf16[512,256]{1,0:T(8,128)(2,1)S(1)}, bf16[512,256]{1,0:T(8,128)(2,1)S(1)}, u32[]{:S(2)}, u32[]{:S(2)}) %collective-permute-start.25) | collective-permute-done | bytes 262176 | tf_op jit(solution)/shard_map/ppermute | solution.py:34
  276.4 2.8 collective-permute-start.28
  279.3 17.2 %collective-permute-done.28 = bf16[256,1536]{1,0:T(8,128)(2,1)S(1)} collective-permute-done((bf16[256,1536]{1,0:T(8,128)(2,1)S(1)}, bf16[256,1536]{1,0:T(8,128)(2,1)S(1)}, u32[]{:S(2)}, u32[]{:S(2)}) %collective-permute-start.28) | collective-permute-done | bytes 786464 | tf_op jit(solution)/shard_map/ppermute | solution.py:26
  (151 shorter events, 66.5 us)
Async XLA Ops:
  7.2 109.0 %all-gather.3.cloned.1.call-start = ((), (), s32[]{:S(2)}) async-start(), calls=%async_computation.2 | async-start | bytes 5898240 | tf_op jit(solution)/shard_map/all_gather | solution.py:242
  8.7 3.1 %collective-permute-start = (bf16[256,1152]{1,0:T(8,128)(2,1)S(1)}, bf16[256,1152]{1,0:T(8,128)(2,1)S(1)}, u32[]{:S(2)}, u32[]{:S(2)}) collective-permute-start(bf16[256,1152]{1,0:T(8,128)(2,1)S(1)} %pad_maximum_fusion.9), channel_id=1, source_target_pairs={{0,8},{8,0},{1,9},{9,1},{2,10},{10,2},{3,11},{11,3},{4,12},{12,4},... | collective-permute-start | bytes 1769480 | tf_op jit(solution)/shard_map/ppermute | solution.py:22
  12.0 16.7 %collective-permute-start.1 = (bf16[256,1152]{1,0:T(8,128)(2,1)S(1)}, bf16[256,1152]{1,0:T(8,128)(2,1)S(1)}, u32[]{:S(2)}, u32[]{:S(2)}) collective-permute-start(bf16[256,1152]{1,0:T(8,128)(2,1)S(1)} %get-tuple-element.115), channel_id=1, source_target_pairs={{0,1},{1,0},{2,3},{3,2},{4,5},{5,4},{6,7},{7,6},{8,9},{9,8},{10,11... | collective-permute-start | bytes 1769480 | tf_op jit(solution)/shard_map/ppermute | solution.py:26
  29.9 131.0 %all-gather.5.cloned.1.call-start = ((), (), s32[]{:S(2)}) async-start(), calls=%async_computation.3 | async-start | bytes 7864320 | tf_op jit(solution)/shard_map/all_gather | solution.py:257
  32.4 18.3 %collective-permute-start.5 = (bf16[256,1536]{1,0:T(8,128)(2,1)S(1)}, bf16[256,1536]{1,0:T(8,128)(2,1)S(1)}, u32[]{:S(2)}, u32[]{:S(2)}) collective-permute-start(bf16[256,1536]{1,0:T(8,128)(2,1)S(1)} %pad_maximum_fusion.7), channel_id=1, source_target_pairs={{0,8},{8,0},{1,9},{9,1},{2,10},{10,2},{3,11},{11,3},{4,12},{12,4},... | collective-permute-start | bytes 2359304 | tf_op jit(solution)/shard_map/ppermute | solution.py:22
  33.2 7.2 %collective-permute-start.2 = (bf16[512,256]{1,0:T(8,128)(2,1)S(1)}, bf16[512,256]{1,0:T(8,128)(2,1)S(1)}, u32[]{:S(2)}, u32[]{:S(2)}) collective-permute-start(bf16[512,256]{1,0:T(8,128)(2,1)S(1)} %copy-done.11), channel_id=1, source_target_pairs={{0,16},{16,0},{1,17},{17,1},{2,18},{18,2},{3,19},{19,3},{4,20},{20... | collective-permute-start | bytes 786440 | tf_op jit(solution)/shard_map/ppermute | solution.py:30
  34.4 13.9 %collective-permute-start.3 = (bf16[512,256]{1,0:T(8,128)(2,1)S(1)}, bf16[512,256]{1,0:T(8,128)(2,1)S(1)}, u32[]{:S(2)}, u32[]{:S(2)}) collective-permute-start(bf16[512,256]{1,0:T(8,128)(2,1)S(1)} %copy-done.11), channel_id=1, source_target_pairs={{0,1},{1,0},{2,3},{3,2},{4,5},{5,4},{6,7},{7,6},{8,9},{9,8},{10,11... | collective-permute-start | bytes 786440 | tf_op jit(solution)/shard_map/ppermute | solution.py:26
  37.0 13.5 %collective-permute-start.4 = (bf16[512,256]{1,0:T(8,128)(2,1)S(1)}, bf16[512,256]{1,0:T(8,128)(2,1)S(1)}, u32[]{:S(2)}, u32[]{:S(2)}) collective-permute-start(bf16[512,256]{1,0:T(8,128)(2,1)S(1)} %copy-done.11), channel_id=1, source_target_pairs={{0,17},{17,0},{1,16},{16,1},{2,19},{19,2},{3,18},{18,3},{4,21},{21... | collective-permute-start | bytes 786440 | tf_op jit(solution)/shard_map/ppermute | solution.py:34
  51.0 18.5 %collective-permute-start.6 = (bf16[256,1536]{1,0:T(8,128)(2,1)S(1)}, bf16[256,1536]{1,0:T(8,128)(2,1)S(1)}, u32[]{:S(2)}, u32[]{:S(2)}) collective-permute-start(bf16[256,1536]{1,0:T(8,128)(2,1)S(1)} %get-tuple-element.58), channel_id=1, source_target_pairs={{0,1},{1,0},{2,3},{3,2},{4,5},{5,4},{6,7},{7,6},{8,9},{9,8},{10,11... | collective-permute-start | bytes 2359304 | tf_op jit(solution)/shard_map/ppermute | solution.py:26
  70.9 161.3 %reduce-scatter.3.cloned.1.call-start = ((), (), s32[]{:S(2)}) async-start(), calls=%async_computation.4 | async-start | bytes 5898240 | tf_op jit(solution)/shard_map/reduce_scatter | solution.py:270
  70.9 23.3 %collective-permute-start.8 = (bf16[1024,512]{1,0:T(8,128)(2,1)S(1)}, bf16[1024,512]{1,0:T(8,128)(2,1)S(1)}, u32[]{:S(2)}, u32[]{:S(2)}) collective-permute-start(bf16[1024,512]{1,0:T(8,128)(2,1)S(1)} %pad_maximum_fusion.2), channel_id=1, source_target_pairs={{0,96},{32,0},{64,32},{96,64},{1,97},{33,1},{65,33},{97,65},{2,98}... | collective-permute-start | bytes 3145736 | tf_op jit(solution)/shard_map/ppermute | solution.py:18
  74.7 22.7 %collective-permute-start.7 = (bf16[1024,512]{1,0:T(8,128)(2,1)S(1)}, bf16[1024,512]{1,0:T(8,128)(2,1)S(1)}, u32[]{:S(2)}, u32[]{:S(2)}) collective-permute-start(bf16[1024,512]{1,0:T(8,128)(2,1)S(1)} %pad_maximum_fusion.2), channel_id=1, source_target_pairs={{0,32},{32,64},{64,96},{96,0},{1,33},{33,65},{65,97},{97,1},{2,34}... | collective-permute-start | bytes 3145736 | tf_op jit(solution)/shard_map/ppermute | solution.py:18
  74.7 27.6 %collective-permute-start.11 = (bf16[4,256,512]{2,1,0:T(8,128)(2,1)}, bf16[4,256,512]{2,1,0:T(8,128)(2,1)}, u32[]{:S(2)}, u32[]{:S(2)}) collective-permute-start(bf16[4,256,512]{2,1,0:T(8,128)(2,1)} %columns.3), channel_id=1, source_target_pairs={{0,17},{17,0},{1,16},{16,1},{2,19},{19,2},{3,18},{18,3},{4,21},{21... | collective-permute-start | bytes 3145736 | tf_op jit(solution)/shard_map/ppermute | solution.py:34
  98.2 10.8 %collective-permute-start.9 = (bf16[512,512]{1,0:T(8,128)(2,1)}, bf16[512,512]{1,0:T(8,128)(2,1)}, u32[]{:S(2)}, u32[]{:S(2)}) collective-permute-start(bf16[512,512]{1,0:T(8,128)(2,1)} %slice.96), channel_id=1, source_target_pairs={{0,32},{32,64},{64,96},{96,0},{1,33},{33,65},{65,97},{97,1},{2,34}... | collective-permute-start | bytes 1572872 | tf_op jit(solution)/shard_map/ppermute | solution.py:18
  99.1 11.9 %collective-permute-start.10 = (bf16[512,512]{1,0:T(8,128)(2,1)}, bf16[512,512]{1,0:T(8,128)(2,1)}, u32[]{:S(2)}, u32[]{:S(2)}) collective-permute-start(bf16[512,512]{1,0:T(8,128)(2,1)} %slice.97), channel_id=1, source_target_pairs={{0,96},{32,0},{64,32},{96,64},{1,97},{33,1},{65,33},{97,65},{2,98}... | collective-permute-start | bytes 1572872 | tf_op jit(solution)/shard_map/ppermute | solution.py:18
  102.4 27.8 %collective-permute-start.12 = (bf16[4,256,512]{2,1,0:T(8,128)(2,1)}, bf16[4,256,512]{2,1,0:T(8,128)(2,1)}, u32[]{:S(2)}, u32[]{:S(2)}) collective-permute-start(bf16[4,256,512]{2,1,0:T(8,128)(2,1)} %collective-permute-done.11), channel_id=1, source_target_pairs={{0,16},{16,0},{1,17},{17,1},{2,18},{18,2},{3,19},{19,3},{4,20},{20... | collective-permute-start | bytes 3145736 | tf_op jit(solution)/shard_map/ppermute | solution.py:30
  125.2 15.2 %collective-permute-start.13 = (bf16[512,768]{1,0:T(8,128)(2,1)}, bf16[512,768]{1,0:T(8,128)(2,1)S(1)}, u32[]{:S(2)}, u32[]{:S(2)}) collective-permute-start(bf16[512,768]{1,0:T(8,128)(2,1)} %get-tuple-element.69), channel_id=1, source_target_pairs={{0,8},{8,0},{1,9},{9,1},{2,10},{10,2},{3,11},{11,3},{4,12},{12,4},... | collective-permute-start | bytes 2359304 | tf_op jit(solution)/shard_map/ppermute | solution.py:22
  145.5 3.1 collective-permute-start.15
  160.6 114.5 %reduce-scatter.5.cloned.1.call-start = ((), (), s32[]{:S(2)}) async-start(), calls=%async_computation.5 | async-start | bytes 7864320 | tf_op jit(solution)/shard_map/reduce_scatter | solution.py:279
  170.1 8.2 %collective-permute-start.16 = (bf16[512,1024]{1,0:T(8,128)(2,1)}, bf16[512,1024]{1,0:T(8,128)(2,1)S(1)}, u32[]{:S(2)}, u32[]{:S(2)}) collective-permute-start(bf16[512,1024]{1,0:T(8,128)(2,1)} %get-tuple-element.76), channel_id=1, source_target_pairs={{0,8},{8,0},{1,9},{9,1},{2,10},{10,2},{3,11},{11,3},{4,12},{12,4},... | collective-permute-start | bytes 3145736 | tf_op jit(solution)/shard_map/ppermute | solution.py:22
  183.9 3.6 %collective-permute-start.18 = (bf16[512,1536]{1,0:T(8,128)(2,1)}, bf16[512,1536]{1,0:T(8,128)(2,1)S(1)}, u32[]{:S(2)}, u32[]{:S(2)}) collective-permute-start(bf16[512,1536]{1,0:T(8,128)(2,1)} %activate.3.mb.dm), channel_id=1, source_target_pairs={{0,8},{8,0},{1,9},{9,1},{2,10},{10,2},{3,11},{11,3},{4,12},{12,4},... | collective-permute-start | bytes 4718600 | tf_op jit(solution)/shard_map/ppermute | solution.py:22
  209.6 14.1 %collective-permute-start.20 = (bf16[512,512]{1,0:T(8,128)(2,1)S(1)}, bf16[512,512]{1,0:T(8,128)(2,1)S(1)}, u32[]{:S(2)}, u32[]{:S(2)}) collective-permute-start(bf16[512,512]{1,0:T(8,128)(2,1)S(1)} %get-tuple-element.116), channel_id=1, source_target_pairs={{0,96},{32,0},{64,32},{96,64},{1,97},{33,1},{65,33},{97,65},{2,98}... | collective-permute-start | bytes 1572872 | tf_op jit(solution)/shard_map/ppermute | solution.py:18
  211.3 14.1 %collective-permute-start.19 = (bf16[512,512]{1,0:T(8,128)(2,1)S(1)}, bf16[512,512]{1,0:T(8,128)(2,1)S(1)}, u32[]{:S(2)}, u32[]{:S(2)}) collective-permute-start(bf16[512,512]{1,0:T(8,128)(2,1)S(1)} %get-tuple-element.117), channel_id=1, source_target_pairs={{0,32},{32,64},{64,96},{96,0},{1,33},{33,65},{65,97},{97,1},{2,34}... | collective-permute-start | bytes 1572872 | tf_op jit(solution)/shard_map/ppermute | solution.py:18
  229.5 24.7 %collective-permute-start.21 = (bf16[1024,512]{1,0:T(8,128)(2,1)}, bf16[1024,512]{1,0:T(8,128)(2,1)S(1)}, u32[]{:S(2)}, u32[]{:S(2)}) collective-permute-start(bf16[1024,512]{1,0:T(8,128)(2,1)} %get-tuple-element.85), channel_id=1, source_target_pairs={{0,32},{32,64},{64,96},{96,0},{1,33},{33,65},{65,97},{97,1},{2,34}... | collective-permute-start | bytes 3145736 | tf_op jit(solution)/shard_map/ppermute | solution.py:18
  229.5 24.7 %collective-permute-start.22 = (bf16[1024,512]{1,0:T(8,128)(2,1)}, bf16[1024,512]{1,0:T(8,128)(2,1)S(1)}, u32[]{:S(2)}, u32[]{:S(2)}) collective-permute-start(bf16[1024,512]{1,0:T(8,128)(2,1)} %get-tuple-element.86), channel_id=1, source_target_pairs={{0,96},{32,0},{64,32},{96,64},{1,97},{33,1},{65,33},{97,65},{2,98}... | collective-permute-start | bytes 3145736 | tf_op jit(solution)/shard_map/ppermute | solution.py:18
  233.6 20.7 %collective-permute-start.23 = (bf16[256,1152]{1,0:T(8,128)(2,1)S(1)}, bf16[256,1152]{1,0:T(8,128)(2,1)S(1)}, u32[]{:S(2)}, u32[]{:S(2)}) collective-permute-start(bf16[256,1152]{1,0:T(8,128)(2,1)S(1)} %get-tuple-element.113), channel_id=1, source_target_pairs={{0,1},{1,0},{2,3},{3,2},{4,5},{5,4},{6,7},{7,6},{8,9},{9,8},{10,11... | collective-permute-start | bytes 1769480 | tf_op jit(solution)/shard_map/ppermute | solution.py:26
  256.1 7.2 %collective-permute-start.26 = (bf16[512,256]{1,0:T(8,128)(2,1)S(1)}, bf16[512,256]{1,0:T(8,128)(2,1)S(1)}, u32[]{:S(2)}, u32[]{:S(2)}) collective-permute-start(bf16[512,256]{1,0:T(8,128)(2,1)S(1)} %slice.152), channel_id=1, source_target_pairs={{0,1},{1,0},{2,3},{3,2},{4,5},{5,4},{6,7},{7,6},{8,9},{9,8},{10,11... | collective-permute-start | bytes 786440 | tf_op jit(solution)/shard_map/ppermute | solution.py:26
  257.1 14.0 %collective-permute-start.25 = (bf16[512,256]{1,0:T(8,128)(2,1)S(1)}, bf16[512,256]{1,0:T(8,128)(2,1)S(1)}, u32[]{:S(2)}, u32[]{:S(2)}) collective-permute-start(bf16[512,256]{1,0:T(8,128)(2,1)S(1)} %get-tuple-element.118), channel_id=1, source_target_pairs={{0,17},{17,0},{1,16},{16,1},{2,19},{19,2},{3,18},{18,3},{4,21},{21... | collective-permute-start | bytes 786440 | tf_op jit(solution)/shard_map/ppermute | solution.py:34
  257.2 13.9 %collective-permute-start.24 = (bf16[512,256]{1,0:T(8,128)(2,1)S(1)}, bf16[512,256]{1,0:T(8,128)(2,1)S(1)}, u32[]{:S(2)}, u32[]{:S(2)}) collective-permute-start(bf16[512,256]{1,0:T(8,128)(2,1)S(1)} %get-tuple-element.119), channel_id=1, source_target_pairs={{0,16},{16,0},{1,17},{17,1},{2,18},{18,2},{3,19},{19,3},{4,20},{20... | collective-permute-start | bytes 786440 | tf_op jit(solution)/shard_map/ppermute | solution.py:30
  271.9 2.5 collective-permute-start.27
  276.4 20.1 %collective-permute-start.28 = (bf16[256,1536]{1,0:T(8,128)(2,1)S(1)}, bf16[256,1536]{1,0:T(8,128)(2,1)S(1)}, u32[]{:S(2)}, u32[]{:S(2)}) collective-permute-start(bf16[256,1536]{1,0:T(8,128)(2,1)S(1)} %slice.111), channel_id=1, source_target_pairs={{0,1},{1,0},{2,3},{3,2},{4,5},{5,4},{6,7},{7,6},{8,9},{9,8},{10,11... | collective-permute-start | bytes 2359304 | tf_op jit(solution)/shard_map/ppermute | solution.py:26
  296.6 3.5 %collective-permute-start.29 = (bf16[256,1536]{1,0:T(8,128)(2,1)S(1)}, bf16[256,1536]{1,0:T(8,128)(2,1)S(1)}, u32[]{:S(2)}, u32[]{:S(2)}) collective-permute-start(bf16[256,1536]{1,0:T(8,128)(2,1)S(1)} %get-tuple-element.101), channel_id=1, source_target_pairs={{0,8},{8,0},{1,9},{9,1},{2,10},{10,2},{3,11},{11,3},{4,12},{12,4},... | collective-permute-start | bytes 2359304 | tf_op jit(solution)/shard_map/ppermute | solution.py:22
  (25 other events, 57.4 us)
Sparse Core Ops, SparseCore 0:
  30.0 54.9 all-gather.2
  86.7 66.0 all-gather.4
  160.7 48.3 reduce-scatter.2
  211.4 63.6 reduce-scatter.4
